TPU v7x, 32 devices: a whole 2x2x4 slice. The times are simulated.
32 devices in a mesh: dp: 4 (over z), seq: 8 (over y, x, core).
Axes of the slice: x: 2, y: 2, z: 4, core: 2. Of those that a mesh axis runs over, the one named last changes fastest.
Arguments:
- queries: bfloat16 [4096, 4096], P(('dp', 'seq')), may hold values from -6 to 6
- keys: bfloat16 [4096, 512], P(('dp', 'seq')), may hold values from -6 to 6
- values: bfloat16 [4096, 512], P(('dp', 'seq')), may hold values from -6 to 6
- grad_out: bfloat16 [4096, 4096], P(('dp', 'seq')), may hold values from -6 to 6
- doc_lengths: int32 [16], replicated, may hold values from 1 to 1024, 4096 in all
Outputs:
- grad_q: bfloat16 [4096, 4096], P(('dp', 'seq'))
- grad_k: bfloat16 [4096, 512], P(('dp', 'seq'))
- grad_v: bfloat16 [4096, 512], P(('dp', 'seq'))
Inputs may be any that keep to these rules, and one draw needn't show every extreme that they name: `doc_lengths`: the 16 lengths sum to 4096; the longest is exactly 1024.
All inputs are finite; a program needn't handle non-finite values.
Results may differ from a plain program's by a relative error of at most 0.0071.
Values may be sent and summed in bfloat16 or wider, within the bound.
No kernel may reach another device: no remote copies, remote signals or barrier semaphores. Data moves between devices by JAX's collectives and lax.ppermute only.
A program may use at most 64 MiB of HBM per device.

v0:
```python
import functools

import jax
import jax.numpy as jnp
from jax import lax
from jax.experimental import pallas as pl
from jax.experimental.pallas import tpu as pltpu
from jax.sharding import PartitionSpec as P

QH = 32
KVH = 4
HD = 128
PER_KV = QH // KVH
LOG2E = 1.4426950408889634
NT = (((1,), (1,)), ((), ()))
NN = (((1,), (0,)), ((), ()))
TN = (((0,), (0,)), ((), ()))


def dot(a, b, dims):
    return lax.dot_general(a, b, dims, preferred_element_type=jnp.float32)


def distance(pair, k, pairs):
    return lax.rem(pair - (pair ^ k) + pairs, pairs)


def attend_kernel(seq_count, info_ref, doc_ref, q_mine, o_mine, qo_theirs, *refs):
    pairs = seq_count // 2
    kv_refs = refs[: pairs + 1]
    dq_mine, dq_theirs, own_out = refs[pairs + 1 : pairs + 4]
    part_outs = refs[pairs + 4 : 2 * pairs + 4]
    kv_all, prob_s, dprob_s, peak_s, stat_s, dq_s, dkv_s = refs[2 * pairs + 4 :]
    tok = q_mine.shape[0]
    keys = 2 * tok
    lanes = PER_KV * tok
    inv_root = HD ** -0.5
    seq_idx = info_ref[1]
    core = lax.rem(seq_idx, 2)
    pair = seq_idx // 2
    chip = info_ref[0] * pairs + pair

    kv_all[0] = kv_refs[0][...]
    kv_all[pairs] = kv_refs[pairs][...]
    for k in range(1, pairs):
        kv_all[distance(pair, k, pairs)] = kv_refs[k][...]
    dkv_s[...] = jnp.zeros_like(dkv_s)
    dq_s[...] = jnp.zeros_like(dq_s)
    stat_s[0] = jnp.full_like(stat_s[0], -1e30)
    stat_s[1] = jnp.zeros_like(stat_s[1])
    stat_s[2] = jnp.zeros_like(stat_s[2])

    row = lax.broadcasted_iota(jnp.int32, (keys, tok), 0)
    row = ((row // tok) ^ core) * tok + lax.rem(row, tok)
    first = chip * keys
    pos = [
        first + (core ^ half) * tok + lax.broadcasted_iota(jnp.int32, (1, tok), 1)
        for half in range(2)
    ]
    starts = [jnp.zeros_like(p) for p in pos]
    low = first * 0
    end = first * 0
    for d in range(doc_ref.shape[0]):
        end = end + doc_ref[d]
        low = jnp.where(first >= end, end, low)
        starts = [jnp.where(p >= end, end, s) for p, s in zip(pos, starts)]
    count = chip - low // keys + 1

    def pieces():
        for half in range(2):
            for c in range(PER_KV // 2):
                yield half, c, pl.ds(half * lanes + c * keys, keys)

    def rows_of(ref, c):
        return jnp.concatenate(
            [ref[:, pl.ds((2 * c + i) * HD, HD)] for i in range(2)], 0
        )

    def q_rows(half, c):
        return rows_of((q_mine, qo_theirs.at[0])[half], c)

    def o_rows(half, c):
        return rows_of((o_mine, qo_theirs.at[1])[half], c)

    def stat_step(back, carry):
        k_tile = kv_all[back, :, pl.ds(0, HD)]
        v_tile = kv_all[back, :, pl.ds(HD, HD)]
        key_pos = (chip - back) * keys + row
        biases = []
        for half in range(2):
            bias = jnp.where((key_pos >= starts[half]) & (key_pos <= pos[half]), 0.0, -1e30)
            biases.append(jnp.concatenate([bias, bias], 1))
        for half, c, cols in pieces():
            peak = stat_s[0, :, cols]
            scores = dot(k_tile, q_rows(half, c), NT) * (inv_root * LOG2E) + biases[half]
            dprobs = dot(v_tile, o_rows(half, c), NT)
            new_peak = jnp.maximum(peak, jnp.max(scores, 0, keepdims=True))
            weights = jnp.exp2(scores - new_peak)
            rescale = jnp.exp2(peak - new_peak)
            stat_s[0, :, cols] = new_peak
            stat_s[1, :, cols] = stat_s[1, :, cols] * rescale + jnp.sum(weights, 0, keepdims=True)
            stat_s[2, :, cols] = stat_s[2, :, cols] * rescale + jnp.sum(
                weights * dprobs, 0, keepdims=True
            )
            prob_s[back, :, cols] = weights
            dprob_s[back, :, cols] = dprobs
            peak_s[back, :, cols] = new_peak
        return carry

    lax.fori_loop(0, count, stat_step, 0)
    inv_total = 1.0 / stat_s[1]
    stat_s[1] = inv_total
    stat_s[2] = stat_s[2] * inv_total

    def grad_step(back, carry):
        k_tile = kv_all[back, :, pl.ds(0, HD)]
        dk = jnp.zeros((keys, HD), jnp.float32)
        dv = jnp.zeros((keys, HD), jnp.float32)
        for half, c, cols in pieces():
            factor = jnp.exp2(peak_s[back, :, cols] - stat_s[0, :, cols]) * stat_s[1, :, cols]
            probs = prob_s[back, :, cols] * factor
            probs_b = probs.astype(jnp.bfloat16)
            dscores = (probs * (dprob_s[back, :, cols] - stat_s[2, :, cols])).astype(jnp.bfloat16)
            dv = dv + dot(probs_b, o_rows(half, c), NN)
            dk = dk + dot(dscores, q_rows(half, c), NN)
            dq_s[:, cols] += dot(k_tile, dscores, TN)
        dkv_s[back, :, pl.ds(0, HD)] = dk * inv_root
        dkv_s[back, :, pl.ds(HD, HD)] = dv
        return carry

    lax.fori_loop(0, count, grad_step, 0)
    own_out[...] = dkv_s[0]
    part_outs[pairs - 1][...] = dkv_s[pairs].astype(jnp.bfloat16)
    for k in range(1, pairs):
        part_outs[k - 1][...] = dkv_s[distance(pair, k, pairs)].astype(jnp.bfloat16)
    for half, dq_ref in enumerate((dq_mine, dq_theirs)):
        for h in range(PER_KV):
            block = dq_s[:, pl.ds(half * lanes + h * tok, tok)] * inv_root
            dq_ref[:, pl.ds(h * HD, HD)] = block.T.astype(jnp.bfloat16)


def attend(g, info, doc_lengths, queries, grad_out, qo_theirs, blocks, seq_count):
    tok = queries.shape[0]
    pairs = seq_count // 2
    lanes = PER_KV * tok
    keys, cols = blocks[0].shape
    width = PER_KV * HD
    dq_shape = jax.ShapeDtypeStruct((tok, width), jnp.bfloat16)
    part = jax.ShapeDtypeStruct((keys, cols), jnp.bfloat16)
    out_shape = [dq_shape, dq_shape, jax.ShapeDtypeStruct((keys, cols), jnp.float32)] + [part] * pairs
    smem = pl.BlockSpec(memory_space=pltpu.SMEM)
    mine = pl.BlockSpec((tok, width), lambda i, info: (0, 2 * lax.rem(info[1], 2) + g))
    whole = pl.BlockSpec((keys, cols), lambda i, info: (0, 0))
    dq_spec = pl.BlockSpec((tok, width), lambda i, info: (0, 0))
    grid_spec = pltpu.PrefetchScalarGridSpec(
        num_scalar_prefetch=1,
        grid=(1,),
        in_specs=[
            smem,
            mine,
            mine,
            pl.BlockSpec((2, tok, width), lambda i, info: (0, 0, g)),
        ]
        + [whole] * len(blocks),
        out_specs=[dq_spec, dq_spec] + [whole] * (pairs + 1),
        scratch_shapes=[
            pltpu.VMEM((pairs + 1, keys, cols), jnp.bfloat16),
            pltpu.VMEM((pairs + 1, keys, 2 * lanes), jnp.float32),
            pltpu.VMEM((pairs + 1, keys, 2 * lanes), jnp.float32),
            pltpu.VMEM((pairs + 1, 1, 2 * lanes), jnp.float32),
            pltpu.VMEM((3, 1, 2 * lanes), jnp.float32),
            pltpu.VMEM((HD, 2 * lanes), jnp.float32),
            pltpu.VMEM((pairs + 1, keys, cols), jnp.float32),
        ],
    )
    return pl.pallas_call(
        functools.partial(attend_kernel, seq_count),
        out_shape=out_shape,
        grid_spec=grid_spec,
        compiler_params=pltpu.CompilerParams(vmem_limit_bytes=56 * 1024 * 1024),
        cost_estimate=pl.CostEstimate(
            flops=10 * keys * 2 * lanes * HD * (pairs + 1),
            bytes_accessed=8 * 1024 * 1024,
            transcendentals=keys * 2 * lanes * (pairs + 1),
        ),
        name="attend_%d" % g,
    )(info, doc_lengths, queries, grad_out, qo_theirs, *blocks)


def local(queries, keys, values, grad_out, doc_lengths):
    tok = queries.shape[0]
    dp_count = lax.axis_size("dp")
    seq_count = lax.axis_size("seq")
    pairs = seq_count // 2
    dp_idx = lax.axis_index("dp")
    seq_idx = lax.axis_index("seq")
    core = lax.rem(seq_idx, 2)
    pair = seq_idx // 2
    groups = KVH // 2

    def swap(value, k):
        return lax.ppermute(value, "seq", [(i, i ^ k) for i in range(seq_count)])

    def kv_half(which):
        return [
            jnp.concatenate(
                [
                    lax.dynamic_slice_in_dim(t, (which * groups + g) * HD, HD, 1)
                    for t in (keys, values)
                ],
                1,
            )
            for g in range(groups)
        ]

    received = swap(jnp.stack(kv_half(1 - core)), 1)
    own = [jnp.concatenate([m, received[g]], 0) for g, m in enumerate(kv_half(core))]
    prev = [
        lax.ppermute(o, "dp", [(i, i + 1) for i in range(dp_count - 1)]) for o in own
    ]
    width = QH // 2 * HD
    qo_theirs = swap(
        jnp.stack(
            [lax.dynamic_slice_in_dim(t, (1 - core) * width, width, 1) for t in (queries, grad_out)]
        ),
        1,
    )
    info = jnp.stack([dp_idx, seq_idx]).astype(jnp.int32)

    blocks = []
    for g in range(groups):
        sent = [swap(jnp.where((pair ^ k) > pair, own[g], prev[g]), 2 * k) for k in range(1, pairs)]
        blocks.append([own[g]] + sent + [prev[g]])
    dq_mine, dq_other, totals = [], [], []
    for g in range(groups):
        outs = attend(g, info, doc_lengths, queries, grad_out, qo_theirs, blocks[g], seq_count)
        dq_mine.append(outs[0])
        dq_other.append(swap(outs[1], 1))
        own_sum = outs[2]
        prev_sum = outs[-1].astype(jnp.float32)
        for k in range(1, pairs):
            back = swap(outs[2 + k], 2 * k).astype(jnp.float32)
            later = (pair ^ k) > pair
            own_sum = own_sum + jnp.where(later, back, 0.0)
            prev_sum = prev_sum + jnp.where(later, 0.0, back)
        from_next = lax.ppermute(
            prev_sum.astype(jnp.bfloat16), "dp", [(i + 1, i) for i in range(dp_count - 1)]
        )
        totals.append((own_sum + from_next.astype(jnp.float32)).astype(jnp.bfloat16))
    mine = [t[:tok] for t in totals]
    other = [swap(t[tok:], 1) for t in totals]

    def join(a, b):
        low = [jnp.where(core == 0, x, y) for x, y in zip(a, b)]
        high = [jnp.where(core == 0, y, x) for x, y in zip(a, b)]
        return jnp.concatenate(low + high, 1)

    grad_q = join(dq_mine, dq_other)
    grad_k = join([m[:, :HD] for m in mine], [o[:, :HD] for o in other])
    grad_v = join([m[:, HD:] for m in mine], [o[:, HD:] for o in other])
    return (grad_q, grad_k, grad_v)


def solution(mesh):
    spec = P(("dp", "seq"), None)
    return jax.shard_map(
        local,
        mesh=mesh,
        in_specs=(spec, spec, spec, spec, P()),
        out_specs=(spec, spec, spec),
        check_vma=False,
    )
```

profile of v0, /device:TPU:0, one launch (start us, length us, event | category | flops | bytes accessed | tf_op | source)
XLA Modules:
  0.0 77.1 jit_solution(15098287279730082891)
XLA Ops:
  0.7 1.0 %constant_dynamic-slice_fusion.6 = (bf16[128,128]{1,0:T(8,128)(2,1)S(1)}, bf16[128,128]{1,0:T(8,128)(2,1)S(1)}, bf16[128,128]{1,0:T(8,128)(2,1)S(1)}, bf16[128,1...) fusion(bf16[128,512]{1,0:T(8,128)(2,1)} %param.7, ...), kind=kLoop, calls=%fused_computation.67 | loop fusion | bytes 524304 | tf_op jit(solution)/shard_map/dynamic_slice | solution.py:208
  2.2 1.1 %dynamic-slice_bitcast_fusion = (bf16[1,128,2048]{2,1,0:T(8,128)(2,1)S(1)}, bf16[1,128,2048]{2,1,0:T(8,128)(2,1)S(1)}) fusion(bf16[128,4096]{1,0:T(8,128)(2,1)} %o_mine.3, s32[]{:T(128)S(6)} %select_n.166, bf16[128,4096]{1,0:T(8,128)(2,1)S(1)} %copy-done), kind=kLoop, calls=%fused_computation.2 | loop fusion | bytes 2097156 | tf_op jit(solution)/shard_map/stack | solution.py:223
  3.8 4.8 %collective-permute-start.2 = (bf16[256,256]{1,0:T(8,128)(2,1)S(1)}, bf16[256,256]{1,0:T(8,128)(2,1)S(1)}, u32[]{:S(2)}, u32[]{:S(2)}) collective-permute-start(bf16[256,256]{1,0:T(8,128)(2,1)S(1)} %pad_maximum_fusion.3.refs_0_), channel_id=1, source_target_pairs={{0,8},{8,16},{16,24},{1,9},{9,17},{17,25},{2,10},{10,18},{18,26},{... | collective-permute-start | bytes 393224 | tf_op jit(solution)/shard_map/ppermute | solution.py:219
  9.2 3.5 %collective-permute-start.7 = (bf16[256,256]{1,0:T(8,128)(2,1)S(1)}, bf16[256,256]{1,0:T(8,128)(2,1)S(1)}, u32[]{:S(2)}, u32[]{:S(2)}) collective-permute-start(bf16[256,256]{1,0:T(8,128)(2,1)S(1)} %pad_maximum_fusion.4.refs_0_), channel_id=1, source_target_pairs={{0,8},{8,16},{16,24},{1,9},{9,17},{17,25},{2,10},{10,18},{18,26},{... | collective-permute-start | bytes 393224 | tf_op jit(solution)/shard_map/ppermute | solution.py:219
  12.8 1.6 %collective-permute-start.3 = (bf16[256,256]{1,0:T(8,128)(2,1)S(1)}, bf16[256,256]{1,0:T(8,128)(2,1)S(1)}, u32[]{:S(2)}, u32[]{:S(2)}) collective-permute-start(bf16[256,256]{1,0:T(8,128)(2,1)S(1)} %get-tuple-element.37), channel_id=1, source_target_pairs={{0,2},{1,3},{2,0},{3,1},{4,6},{5,7},{6,4},{7,5},{8,10},{9,11},{10,... | collective-permute-start | bytes 393224 | tf_op jit(solution)/shard_map/ppermute | solution.py:202
  14.4 1.5 %collective-permute-start.4 = (bf16[256,256]{1,0:T(8,128)(2,1)S(1)}, bf16[256,256]{1,0:T(8,128)(2,1)S(1)}, u32[]{:S(2)}, u32[]{:S(2)}) collective-permute-start(bf16[256,256]{1,0:T(8,128)(2,1)S(1)} %get-tuple-element.36), channel_id=1, source_target_pairs={{0,4},{1,5},{2,6},{3,7},{4,0},{5,1},{6,2},{7,3},{8,12},{9,13},{10,... | collective-permute-start | bytes 393224 | tf_op jit(solution)/shard_map/ppermute | solution.py:202
  16.4 2.5 %collective-permute-start.10 = (bf16[256,256]{1,0:T(8,128)(2,1)S(1)}, bf16[256,256]{1,0:T(8,128)(2,1)S(1)}, u32[]{:S(2)}, u32[]{:S(2)}) collective-permute-start(bf16[256,256]{1,0:T(8,128)(2,1)S(1)} %get-tuple-element.38), channel_id=1, source_target_pairs={{0,6},{1,7},{2,4},{3,5},{4,2},{5,3},{6,0},{7,1},{8,14},{9,15},{10,... | collective-permute-start | bytes 393224 | tf_op jit(solution)/shard_map/ppermute | solution.py:202
  18.9 1.8 %collective-permute-start.8 = (bf16[256,256]{1,0:T(8,128)(2,1)S(1)}, bf16[256,256]{1,0:T(8,128)(2,1)S(1)}, u32[]{:S(2)}, u32[]{:S(2)}) collective-permute-start(bf16[256,256]{1,0:T(8,128)(2,1)S(1)} %get-tuple-element.40), channel_id=1, source_target_pairs={{0,2},{1,3},{2,0},{3,1},{4,6},{5,7},{6,4},{7,5},{8,10},{9,11},{10,... | collective-permute-start | bytes 393224 | tf_op jit(solution)/shard_map/ppermute | solution.py:202
  20.8 4.2 %collective-permute-done.4.refs_2_ = bf16[256,256]{1,0:T(8,128)(2,1)S(1)} collective-permute-done((bf16[256,256]{1,0:T(8,128)(2,1)S(1)}, bf16[256,256]{1,0:T(8,128)(2,1)S(1)}, u32[]{:S(2)}, u32[]{:S(2)}) %collective-permute-start.4) | collective-permute-done | bytes 131104 | tf_op jit(solution)/shard_map/ppermute | solution.py:202
  24.9 2.5 %collective-permute-start.9 = (bf16[256,256]{1,0:T(8,128)(2,1)S(1)}, bf16[256,256]{1,0:T(8,128)(2,1)S(1)}, u32[]{:S(2)}, u32[]{:S(2)}) collective-permute-start(bf16[256,256]{1,0:T(8,128)(2,1)S(1)} %get-tuple-element.39), channel_id=1, source_target_pairs={{0,4},{1,5},{2,6},{3,7},{4,0},{5,1},{6,2},{7,3},{8,12},{9,13},{10,... | collective-permute-start | bytes 393224 | tf_op jit(solution)/shard_map/ppermute | solution.py:202
  29.0 5.5 %attend_0.1 = (bf16[128,1024]{1,0:T(8,128)(2,1)}, bf16[128,1024]{1,0:T(8,128)(2,1)}, f32[256,256]{1,0:T(8,128)}, bf16[256,256]{1,0:T(8,128)(2,1)}, bf16[256,256]...) custom-call(s32[2]{0:T(128)} %pad_add_fusion.info_ref, s32[16]{0:T(128)} %doc_ref.3, ...), custom_call_target="tpu_custom_call" | custom-call | flops 3355443200 | bytes 8388608 | tf_op jit(solution)/shard_map/attend_0/pallas_call | solution.py:176
  35.0 1.6 %collective-permute-start.13 = (bf16[256,256]{1,0:T(8,128)(2,1)}, bf16[256,256]{1,0:T(8,128)(2,1)S(1)}, u32[]{:S(2)}, u32[]{:S(2)}) collective-permute-start(bf16[256,256]{1,0:T(8,128)(2,1)} %get-tuple-element.23), channel_id=1, source_target_pairs={{0,4},{1,5},{2,6},{3,7},{4,0},{5,1},{6,2},{7,3},{8,12},{9,13},{10,... | collective-permute-start | bytes 393224 | tf_op jit(solution)/shard_map/ppermute | solution.py:202
  36.6 1.6 %collective-permute-start.14 = (bf16[256,256]{1,0:T(8,128)(2,1)}, bf16[256,256]{1,0:T(8,128)(2,1)S(1)}, u32[]{:S(2)}, u32[]{:S(2)}) collective-permute-start(bf16[256,256]{1,0:T(8,128)(2,1)} %get-tuple-element.24), channel_id=1, source_target_pairs={{0,6},{1,7},{2,4},{3,5},{4,2},{5,3},{6,0},{7,1},{8,14},{9,15},{10,... | collective-permute-start | bytes 393224 | tf_op jit(solution)/shard_map/ppermute | solution.py:202
  39.5 5.4 %attend_1.1 = (bf16[128,1024]{1,0:T(8,128)(2,1)}, bf16[128,1024]{1,0:T(8,128)(2,1)}, f32[256,256]{1,0:T(8,128)}, bf16[256,256]{1,0:T(8,128)(2,1)}, bf16[256,256]...) custom-call(s32[2]{0:T(128)} %pad_add_fusion.info_ref, s32[16]{0:T(128)} %doc_ref.3, ...), custom_call_target="tpu_custom_call" | custom-call | flops 3355443200 | bytes 8388608 | tf_op jit(solution)/shard_map/attend_1/pallas_call | solution.py:176
  44.9 2.4 %collective-permute-start.17 = (bf16[256,256]{1,0:T(8,128)(2,1)}, bf16[256,256]{1,0:T(8,128)(2,1)S(1)}, u32[]{:S(2)}, u32[]{:S(2)}) collective-permute-start(bf16[256,256]{1,0:T(8,128)(2,1)} %get-tuple-element.27), channel_id=1, source_target_pairs={{0,2},{1,3},{2,0},{3,1},{4,6},{5,7},{6,4},{7,5},{8,10},{9,11},{10,... | collective-permute-start | bytes 393224 | tf_op jit(solution)/shard_map/ppermute | solution.py:202
  47.4 1.5 %collective-permute-start.18 = (bf16[256,256]{1,0:T(8,128)(2,1)}, bf16[256,256]{1,0:T(8,128)(2,1)S(1)}, u32[]{:S(2)}, u32[]{:S(2)}) collective-permute-start(bf16[256,256]{1,0:T(8,128)(2,1)} %get-tuple-element.28), channel_id=1, source_target_pairs={{0,4},{1,5},{2,6},{3,7},{4,0},{5,1},{6,2},{7,3},{8,12},{9,13},{10,... | collective-permute-start | bytes 393224 | tf_op jit(solution)/shard_map/ppermute | solution.py:202
  48.9 1.4 %collective-permute-start.19 = (bf16[256,256]{1,0:T(8,128)(2,1)}, bf16[256,256]{1,0:T(8,128)(2,1)S(1)}, u32[]{:S(2)}, u32[]{:S(2)}) collective-permute-start(bf16[256,256]{1,0:T(8,128)(2,1)} %get-tuple-element.29), channel_id=1, source_target_pairs={{0,6},{1,7},{2,4},{3,5},{4,2},{5,3},{6,0},{7,1},{8,14},{9,15},{10,... | collective-permute-start | bytes 393224 | tf_op jit(solution)/shard_map/ppermute | solution.py:202
  50.9 1.3 %collective-permute-start.15 = (bf16[256,256]{1,0:T(8,128)(2,1)S(1)}, bf16[256,256]{1,0:T(8,128)(2,1)S(1)}, u32[]{:S(2)}, u32[]{:S(2)}) collective-permute-start(bf16[256,256]{1,0:T(8,128)(2,1)S(1)} %fusion.8), channel_id=1, source_target_pairs={{8,0},{16,8},{24,16},{9,1},{17,9},{25,17},{10,2},{18,10},{26,18},{... | collective-permute-start | bytes 393224 | tf_op jit(solution)/shard_map/ppermute | solution.py:246
  52.5 2.4 %collective-permute-done.19 = bf16[256,256]{1,0:T(8,128)(2,1)S(1)} collective-permute-done((bf16[256,256]{1,0:T(8,128)(2,1)}, bf16[256,256]{1,0:T(8,128)(2,1)S(1)}, u32[]{:S(2)}, u32[]{:S(2)}) %collective-permute-start.19) | collective-permute-done | bytes 131104 | tf_op jit(solution)/shard_map/ppermute | solution.py:202
  55.0 1.0 %fusion.17 = bf16[256,256]{1,0:T(8,128)(2,1)S(1)} fusion(bf16[256,256]{1,0:T(8,128)(2,1)S(1)} %collective-permute-done.17, bf16[256,256]{1,0:T(8,128)(2,1)S(1)} %collective-permute-done.18, bf16[256,256]{1,0:T(8,128)(2,1)S(1)} %collective-permute-done.19, bf16[256,256]{1,0:T(8,128)(2,1)} %get-tuple-element.30, pred[]{:T(512)S(6)} %gt.8, pred[]{:T(512)S(6)} %gt.7, ...), kind=kLoop, calls=%fused_computation.33 | loop fusion | flops 720896 | bytes 655363 | tf_op jit(solution)/shard_map/convert_element_type | solution.py:247
  56.0 1.3 %collective-permute-start.20 = (bf16[256,256]{1,0:T(8,128)(2,1)S(1)}, bf16[256,256]{1,0:T(8,128)(2,1)S(1)}, u32[]{:S(2)}, u32[]{:S(2)}) collective-permute-start(bf16[256,256]{1,0:T(8,128)(2,1)S(1)} %fusion.17), channel_id=1, source_target_pairs={{8,0},{16,8},{24,16},{9,1},{17,9},{25,17},{10,2},{18,10},{26,18},{... | collective-permute-start | bytes 393224 | tf_op jit(solution)/shard_map/ppermute | solution.py:246
  57.3 12.1 %collective-permute-done.15 = bf16[256,256]{1,0:T(8,128)(2,1)S(1)} collective-permute-done((bf16[256,256]{1,0:T(8,128)(2,1)S(1)}, bf16[256,256]{1,0:T(8,128)(2,1)S(1)}, u32[]{:S(2)}, u32[]{:S(2)}) %collective-permute-start.15) | collective-permute-done | bytes 131104 | tf_op jit(solution)/shard_map/ppermute | solution.py:246
  69.6 4.0 %collective-permute-done.20 = bf16[256,256]{1,0:T(8,128)(2,1)S(1)} collective-permute-done((bf16[256,256]{1,0:T(8,128)(2,1)S(1)}, bf16[256,256]{1,0:T(8,128)(2,1)S(1)}, u32[]{:S(2)}, u32[]{:S(2)}) %collective-permute-start.20) | collective-permute-done | bytes 131104 | tf_op jit(solution)/shard_map/ppermute | solution.py:246
  74.7 1.0 %pad_maximum_fusion.1 = bf16[128,4096]{1,0:T(8,128)(2,1)} fusion(bf16[128,1024]{1,0:T(8,128)(2,1)S(1)} %get-tuple-element.34, bf16[128,1024]{1,0:T(8,128)(2,1)S(1)} %get-tuple-element.32, bf16[128,1024]{1,0:T(8,128)(2,1)S(1)} %get-tuple-element.33, bf16[128,1024]{1,0:T(8,128)(2,1)S(1)} %get-tuple-element.31), kind=kLoop, calls=%fused_computation.1 | loop fusion | flops 4194304 | bytes 2097152 | tf_op jit(solution)/shard_map/concatenate | solution.py:256
  (83 shorter events, 9.1 us)
Async XLA Ops:
  1.7 2.0 %collective-permute-start.1 = (bf16[2,128,256]{2,1,0:T(8,128)(2,1)S(1)}, bf16[2,128,256]{2,1,0:T(8,128)(2,1)S(1)}, u32[]{:S(2)}, u32[]{:S(2)}) collective-permute-start(bf16[2,128,256]{2,1,0:T(8,128)(2,1)S(1)} %pad_maximum_fusion.2), channel_id=1, source_target_pairs={{0,1},{1,0},{2,3},{3,2},{4,5},{5,4},{6,7},{7,6},{8,9},{9,8},{10,11... | collective-permute-start | bytes 393224 | tf_op jit(solution)/shard_map/ppermute | solution.py:202
  3.5 24.0 %collective-permute-start = (bf16[2,128,2048]{2,1,0:T(8,128)(2,1)S(1)}, bf16[2,128,2048]{2,1,0:T(8,128)(2,1)S(1)}, u32[]{:S(2)}, u32[]{:S(2)}) collective-permute-start(bf16[2,128,2048]{2,1,0:T(8,128)(2,1)S(1)} %pad_maximum_fusion), channel_id=1, source_target_pairs={{0,1},{1,0},{2,3},{3,2},{4,5},{5,4},{6,7},{7,6},{8,9},{9,8},{10,11... | collective-permute-start | bytes 3145736 | tf_op jit(solution)/shard_map/ppermute | solution.py:202
  3.8 8.9 %collective-permute-start.2 = (bf16[256,256]{1,0:T(8,128)(2,1)S(1)}, bf16[256,256]{1,0:T(8,128)(2,1)S(1)}, u32[]{:S(2)}, u32[]{:S(2)}) collective-permute-start(bf16[256,256]{1,0:T(8,128)(2,1)S(1)} %pad_maximum_fusion.3.refs_0_), channel_id=1, source_target_pairs={{0,8},{8,16},{16,24},{1,9},{9,17},{17,25},{2,10},{10,18},{18,26},{... | collective-permute-start | bytes 393224 | tf_op jit(solution)/shard_map/ppermute | solution.py:219
  9.2 25.3 %copy-start.6 = (bf16[256,256]{1,0:T(8,128)(2,1)}, bf16[256,256]{1,0:T(8,128)(2,1)S(1)}, u32[]{:S(2)}) copy-start(bf16[256,256]{1,0:T(8,128)(2,1)S(1)} %pad_maximum_fusion.4.refs_0_) | copy-start | bytes 393220
  9.2 7.1 %collective-permute-start.7 = (bf16[256,256]{1,0:T(8,128)(2,1)S(1)}, bf16[256,256]{1,0:T(8,128)(2,1)S(1)}, u32[]{:S(2)}, u32[]{:S(2)}) collective-permute-start(bf16[256,256]{1,0:T(8,128)(2,1)S(1)} %pad_maximum_fusion.4.refs_0_), channel_id=1, source_target_pairs={{0,8},{8,16},{16,24},{1,9},{9,17},{17,25},{2,10},{10,18},{18,26},{... | collective-permute-start | bytes 393224 | tf_op jit(solution)/shard_map/ppermute | solution.py:219
  12.8 6.1 %collective-permute-start.3 = (bf16[256,256]{1,0:T(8,128)(2,1)S(1)}, bf16[256,256]{1,0:T(8,128)(2,1)S(1)}, u32[]{:S(2)}, u32[]{:S(2)}) collective-permute-start(bf16[256,256]{1,0:T(8,128)(2,1)S(1)} %get-tuple-element.37), channel_id=1, source_target_pairs={{0,2},{1,3},{2,0},{3,1},{4,6},{5,7},{6,4},{7,5},{8,10},{9,11},{10,... | collective-permute-start | bytes 393224 | tf_op jit(solution)/shard_map/ppermute | solution.py:202
  14.4 10.6 %collective-permute-start.4 = (bf16[256,256]{1,0:T(8,128)(2,1)S(1)}, bf16[256,256]{1,0:T(8,128)(2,1)S(1)}, u32[]{:S(2)}, u32[]{:S(2)}) collective-permute-start(bf16[256,256]{1,0:T(8,128)(2,1)S(1)} %get-tuple-element.36), channel_id=1, source_target_pairs={{0,4},{1,5},{2,6},{3,7},{4,0},{5,1},{6,2},{7,3},{8,12},{9,13},{10,... | collective-permute-start | bytes 393224 | tf_op jit(solution)/shard_map/ppermute | solution.py:202
  15.9 11.6 %collective-permute-start.5 = (bf16[256,256]{1,0:T(8,128)(2,1)S(1)}, bf16[256,256]{1,0:T(8,128)(2,1)S(1)}, u32[]{:S(2)}, u32[]{:S(2)}) collective-permute-start(bf16[256,256]{1,0:T(8,128)(2,1)S(1)} %get-tuple-element.35), channel_id=1, source_target_pairs={{0,6},{1,7},{2,4},{3,5},{4,2},{5,3},{6,0},{7,1},{8,14},{9,15},{10,... | collective-permute-start | bytes 393224 | tf_op jit(solution)/shard_map/ppermute | solution.py:202
  16.4 20.2 %collective-permute-start.10 = (bf16[256,256]{1,0:T(8,128)(2,1)S(1)}, bf16[256,256]{1,0:T(8,128)(2,1)S(1)}, u32[]{:S(2)}, u32[]{:S(2)}) collective-permute-start(bf16[256,256]{1,0:T(8,128)(2,1)S(1)} %get-tuple-element.38), channel_id=1, source_target_pairs={{0,6},{1,7},{2,4},{3,5},{4,2},{5,3},{6,0},{7,1},{8,14},{9,15},{10,... | collective-permute-start | bytes 393224 | tf_op jit(solution)/shard_map/ppermute | solution.py:202
  18.9 19.2 %collective-permute-start.8 = (bf16[256,256]{1,0:T(8,128)(2,1)S(1)}, bf16[256,256]{1,0:T(8,128)(2,1)S(1)}, u32[]{:S(2)}, u32[]{:S(2)}) collective-permute-start(bf16[256,256]{1,0:T(8,128)(2,1)S(1)} %get-tuple-element.40), channel_id=1, source_target_pairs={{0,2},{1,3},{2,0},{3,1},{4,6},{5,7},{6,4},{7,5},{8,10},{9,11},{10,... | collective-permute-start | bytes 393224 | tf_op jit(solution)/shard_map/ppermute | solution.py:202
  24.9 13.2 %collective-permute-start.9 = (bf16[256,256]{1,0:T(8,128)(2,1)S(1)}, bf16[256,256]{1,0:T(8,128)(2,1)S(1)}, u32[]{:S(2)}, u32[]{:S(2)}) collective-permute-start(bf16[256,256]{1,0:T(8,128)(2,1)S(1)} %get-tuple-element.39), channel_id=1, source_target_pairs={{0,4},{1,5},{2,6},{3,7},{4,0},{5,1},{6,2},{7,3},{8,12},{9,13},{10,... | collective-permute-start | bytes 393224 | tf_op jit(solution)/shard_map/ppermute | solution.py:202
  34.5 14.3 %collective-permute-start.12 = (bf16[256,256]{1,0:T(8,128)(2,1)}, bf16[256,256]{1,0:T(8,128)(2,1)S(1)}, u32[]{:S(2)}, u32[]{:S(2)}) collective-permute-start(bf16[256,256]{1,0:T(8,128)(2,1)} %get-tuple-element.22), channel_id=1, source_target_pairs={{0,2},{1,3},{2,0},{3,1},{4,6},{5,7},{6,4},{7,5},{8,10},{9,11},{10,... | collective-permute-start | bytes 393224 | tf_op jit(solution)/shard_map/ppermute | solution.py:202
  35.0 15.2 %collective-permute-start.13 = (bf16[256,256]{1,0:T(8,128)(2,1)}, bf16[256,256]{1,0:T(8,128)(2,1)S(1)}, u32[]{:S(2)}, u32[]{:S(2)}) collective-permute-start(bf16[256,256]{1,0:T(8,128)(2,1)} %get-tuple-element.23), channel_id=1, source_target_pairs={{0,4},{1,5},{2,6},{3,7},{4,0},{5,1},{6,2},{7,3},{8,12},{9,13},{10,... | collective-permute-start | bytes 393224 | tf_op jit(solution)/shard_map/ppermute | solution.py:202
  36.6 13.7 %collective-permute-start.14 = (bf16[256,256]{1,0:T(8,128)(2,1)}, bf16[256,256]{1,0:T(8,128)(2,1)S(1)}, u32[]{:S(2)}, u32[]{:S(2)}) collective-permute-start(bf16[256,256]{1,0:T(8,128)(2,1)} %get-tuple-element.24), channel_id=1, source_target_pairs={{0,6},{1,7},{2,4},{3,5},{4,2},{5,3},{6,0},{7,1},{8,14},{9,15},{10,... | collective-permute-start | bytes 393224 | tf_op jit(solution)/shard_map/ppermute | solution.py:202
  44.9 24.5 %copy-start.3 = (f32[256,256]{1,0:T(8,128)S(1)}, f32[256,256]{1,0:T(8,128)}, u32[]{:S(2)}) copy-start(f32[256,256]{1,0:T(8,128)} %get-tuple-element.21) | copy-start | bytes 786436
  44.9 6.0 %collective-permute-start.17 = (bf16[256,256]{1,0:T(8,128)(2,1)}, bf16[256,256]{1,0:T(8,128)(2,1)S(1)}, u32[]{:S(2)}, u32[]{:S(2)}) collective-permute-start(bf16[256,256]{1,0:T(8,128)(2,1)} %get-tuple-element.27), channel_id=1, source_target_pairs={{0,2},{1,3},{2,0},{3,1},{4,6},{5,7},{6,4},{7,5},{8,10},{9,11},{10,... | collective-permute-start | bytes 393224 | tf_op jit(solution)/shard_map/ppermute | solution.py:202
  47.4 5.2 %collective-permute-start.18 = (bf16[256,256]{1,0:T(8,128)(2,1)}, bf16[256,256]{1,0:T(8,128)(2,1)S(1)}, u32[]{:S(2)}, u32[]{:S(2)}) collective-permute-start(bf16[256,256]{1,0:T(8,128)(2,1)} %get-tuple-element.28), channel_id=1, source_target_pairs={{0,4},{1,5},{2,6},{3,7},{4,0},{5,1},{6,2},{7,3},{8,12},{9,13},{10,... | collective-permute-start | bytes 393224 | tf_op jit(solution)/shard_map/ppermute | solution.py:202
  48.9 6.1 %collective-permute-start.19 = (bf16[256,256]{1,0:T(8,128)(2,1)}, bf16[256,256]{1,0:T(8,128)(2,1)S(1)}, u32[]{:S(2)}, u32[]{:S(2)}) collective-permute-start(bf16[256,256]{1,0:T(8,128)(2,1)} %get-tuple-element.29), channel_id=1, source_target_pairs={{0,6},{1,7},{2,4},{3,5},{4,2},{5,3},{6,0},{7,1},{8,14},{9,15},{10,... | collective-permute-start | bytes 393224 | tf_op jit(solution)/shard_map/ppermute | solution.py:202
  50.3 23.6 %collective-permute-start.6 = (bf16[128,1024]{1,0:T(8,128)(2,1)S(1)}, bf16[128,1024]{1,0:T(8,128)(2,1)S(1)}, u32[]{:S(2)}, u32[]{:S(2)}) collective-permute-start(bf16[128,1024]{1,0:T(8,128)(2,1)S(1)} %copy-done.11), channel_id=1, source_target_pairs={{0,1},{1,0},{2,3},{3,2},{4,5},{5,4},{6,7},{7,6},{8,9},{9,8},{10,11... | collective-permute-start | bytes 786440 | tf_op jit(solution)/shard_map/ppermute | solution.py:202
  50.3 23.7 %collective-permute-start.11 = (bf16[128,1024]{1,0:T(8,128)(2,1)}, bf16[128,1024]{1,0:T(8,128)(2,1)S(1)}, u32[]{:S(2)}, u32[]{:S(2)}) collective-permute-start(bf16[128,1024]{1,0:T(8,128)(2,1)} %get-tuple-element.20), channel_id=1, source_target_pairs={{0,1},{1,0},{2,3},{3,2},{4,5},{5,4},{6,7},{7,6},{8,9},{9,8},{10,11... | collective-permute-start | bytes 786440 | tf_op jit(solution)/shard_map/ppermute | solution.py:202
  50.9 18.5 %collective-permute-start.15 = (bf16[256,256]{1,0:T(8,128)(2,1)S(1)}, bf16[256,256]{1,0:T(8,128)(2,1)S(1)}, u32[]{:S(2)}, u32[]{:S(2)}) collective-permute-start(bf16[256,256]{1,0:T(8,128)(2,1)S(1)} %fusion.8), channel_id=1, source_target_pairs={{8,0},{16,8},{24,16},{9,1},{17,9},{25,17},{10,2},{18,10},{26,18},{... | collective-permute-start | bytes 393224 | tf_op jit(solution)/shard_map/ppermute | solution.py:246
  56.0 17.7 %collective-permute-start.20 = (bf16[256,256]{1,0:T(8,128)(2,1)S(1)}, bf16[256,256]{1,0:T(8,128)(2,1)S(1)}, u32[]{:S(2)}, u32[]{:S(2)}) collective-permute-start(bf16[256,256]{1,0:T(8,128)(2,1)S(1)} %fusion.17), channel_id=1, source_target_pairs={{8,0},{16,8},{24,16},{9,1},{17,9},{25,17},{10,2},{18,10},{26,18},{... | collective-permute-start | bytes 393224 | tf_op jit(solution)/shard_map/ppermute | solution.py:246
  69.6 6.2 %collective-permute-start.16 = (bf16[128,256]{1,0:T(8,128)(2,1)S(1)}, bf16[128,256]{1,0:T(8,128)(2,1)S(1)}, u32[]{:S(2)}, u32[]{:S(2)}) collective-permute-start(bf16[128,256]{1,0:T(8,128)(2,1)S(1)} %slice.57), channel_id=1, source_target_pairs={{0,1},{1,0},{2,3},{3,2},{4,5},{5,4},{6,7},{7,6},{8,9},{9,8},{10,11... | collective-permute-start | bytes 196616 | tf_op jit(solution)/shard_map/ppermute | solution.py:202
  73.8 1.9 %collective-permute-start.21 = (bf16[128,256]{1,0:T(8,128)(2,1)S(1)}, bf16[128,256]{1,0:T(8,128)(2,1)S(1)}, u32[]{:S(2)}, u32[]{:S(2)}) collective-permute-start(bf16[128,256]{1,0:T(8,128)(2,1)S(1)} %slice.60), channel_id=1, source_target_pairs={{0,1},{1,0},{2,3},{3,2},{4,5},{5,4},{6,7},{7,6},{8,9},{9,8},{10,11... | collective-permute-start | bytes 196616 | tf_op jit(solution)/shard_map/ppermute | solution.py:202
  (16 other events, 129.9 us)
where the time goes:
time: 77.5 us; the launch traced here: 77.1 us
  starting transfers between devices  31.6 us (41%)
  waiting for transfers between devices  23.2 us (30%)
  Pallas kernels  10.9 us (14%)
  local copies, waits for them, and re-layouts  5.71 us (7%)
  other arithmetic  4.7 us (6%)
  between operations  1 us (1%)
    ppermute x18, starting transfers between devices, swap(): return lax.ppermute(value, 'seq', [(i, i ^ k) for i in range(seq_count)])  20.8 us
    ppermute x2, waiting for transfers between devices, local(): lax.ppermute(prev_sum.astype(jnp.bfloat16), 'dp', [(i + 1, i) for i in ra...  16.2 us
    pallas_call x2, Pallas kernels, attend(): pl.pallas_call(functools.partial(attend_kernel, seq_count), out_shape=out...  10.9 us
    ppermute x2, starting transfers between devices, local(): lax.ppermute(o, 'dp', [(i, i + 1) for i in range(dp_count - 1)])  8.27 us
    ppermute x18, waiting for transfers between devices, swap(): return lax.ppermute(value, 'seq', [(i, i ^ k) for i in range(seq_count)])  6.98 us
    unnamed x36, local copies, waits for them, and re-layouts  3.58 us
    ppermute x2, starting transfers between devices, local(): lax.ppermute(prev_sum.astype(jnp.bfloat16), 'dp', [(i + 1, i) for i in ra...  2.58 us
    concatenate x3, other arithmetic, join(): return jnp.concatenate(low + high, 1)  2.39 us
  transfers between devices with their start and end apart: 22, of which 5 were waited for; matrix products, arithmetic and copies ran while one was open for 6% of the time, Pallas kernels for 14%

commit v1 on v0

--- a/solution.py
+++ b/solution.py
@@ -25,7 +25,7 @@
     return lax.rem(pair - (pair ^ k) + pairs, pairs)
 
 
-def attend_kernel(seq_count, info_ref, doc_ref, q_mine, o_mine, qo_theirs, *refs):
+def attend_kernel(g, seq_count, info_ref, doc_ref, q_mine, o_mine, qo_theirs, *refs):
     pairs = seq_count // 2
     kv_refs = refs[: pairs + 1]
     dq_mine, dq_theirs, own_out = refs[pairs + 1 : pairs + 4]
@@ -34,6 +34,7 @@
     tok = q_mine.shape[0]
     keys = 2 * tok
     lanes = PER_KV * tok
+    width = lanes // tok * HD
     inv_root = HD ** -0.5
     seq_idx = info_ref[1]
     core = lax.rem(seq_idx, 2)
@@ -71,16 +72,18 @@
             for c in range(PER_KV // 2):
                 yield half, c, pl.ds(half * lanes + c * keys, keys)
 
-    def rows_of(ref, c):
+    def rows_of(ref, offset, c):
         return jnp.concatenate(
-            [ref[:, pl.ds((2 * c + i) * HD, HD)] for i in range(2)], 0
+            [ref[:, pl.ds(offset + (2 * c + i) * HD, HD)] for i in range(2)], 0
         )
 
+    mine_at = pl.multiple_of((core * (KVH // 2) + g) * width, HD)
+
     def q_rows(half, c):
-        return rows_of((q_mine, qo_theirs.at[0])[half], c)
+        return rows_of(q_mine, mine_at, c) if half == 0 else rows_of(qo_theirs.at[0], g * width, c)
 
     def o_rows(half, c):
-        return rows_of((o_mine, qo_theirs.at[1])[half], c)
+        return rows_of(o_mine, mine_at, c) if half == 0 else rows_of(qo_theirs.at[1], g * width, c)
 
     def stat_step(back, carry):
         k_tile = kv_all[back, :, pl.ds(0, HD)]
@@ -149,35 +152,25 @@
     part = jax.ShapeDtypeStruct((keys, cols), jnp.bfloat16)
     out_shape = [dq_shape, dq_shape, jax.ShapeDtypeStruct((keys, cols), jnp.float32)] + [part] * pairs
     smem = pl.BlockSpec(memory_space=pltpu.SMEM)
-    mine = pl.BlockSpec((tok, width), lambda i, info: (0, 2 * lax.rem(info[1], 2) + g))
-    whole = pl.BlockSpec((keys, cols), lambda i, info: (0, 0))
-    dq_spec = pl.BlockSpec((tok, width), lambda i, info: (0, 0))
-    grid_spec = pltpu.PrefetchScalarGridSpec(
-        num_scalar_prefetch=1,
-        grid=(1,),
-        in_specs=[
-            smem,
-            mine,
-            mine,
-            pl.BlockSpec((2, tok, width), lambda i, info: (0, 0, g)),
-        ]
-        + [whole] * len(blocks),
-        out_specs=[dq_spec, dq_spec] + [whole] * (pairs + 1),
+    vmem = pl.BlockSpec(memory_space=pltpu.VMEM)
+    slots = pairs + 1
+    scratch = 8 * slots * keys * 2 * lanes + 4 * HD * 2 * lanes + 10 * slots * keys * cols
+    operands = 12 * tok * QH * HD + 8 * slots * keys * cols
+    return pl.pallas_call(
+        functools.partial(attend_kernel, g, seq_count),
+        out_shape=out_shape,
+        in_specs=[smem, smem] + [vmem] * (3 + len(blocks)),
+        out_specs=[vmem] * len(out_shape),
         scratch_shapes=[
-            pltpu.VMEM((pairs + 1, keys, cols), jnp.bfloat16),
-            pltpu.VMEM((pairs + 1, keys, 2 * lanes), jnp.float32),
-            pltpu.VMEM((pairs + 1, keys, 2 * lanes), jnp.float32),
-            pltpu.VMEM((pairs + 1, 1, 2 * lanes), jnp.float32),
+            pltpu.VMEM((slots, keys, cols), jnp.bfloat16),
+            pltpu.VMEM((slots, keys, 2 * lanes), jnp.float32),
+            pltpu.VMEM((slots, keys, 2 * lanes), jnp.float32),
+            pltpu.VMEM((slots, 1, 2 * lanes), jnp.float32),
             pltpu.VMEM((3, 1, 2 * lanes), jnp.float32),
             pltpu.VMEM((HD, 2 * lanes), jnp.float32),
-            pltpu.VMEM((pairs + 1, keys, cols), jnp.float32),
+            pltpu.VMEM((slots, keys, cols), jnp.float32),
         ],
-    )
-    return pl.pallas_call(
-        functools.partial(attend_kernel, seq_count),
-        out_shape=out_shape,
-        grid_spec=grid_spec,
-        compiler_params=pltpu.CompilerParams(vmem_limit_bytes=56 * 1024 * 1024),
+        compiler_params=pltpu.CompilerParams(vmem_limit_bytes=scratch + operands + 4 * 1024 * 1024),
         cost_estimate=pl.CostEstimate(
             flops=10 * keys * 2 * lanes * HD * (pairs + 1),
             bytes_accessed=8 * 1024 * 1024,

time: 77.5 us -> 68.8 us (0.89); the launches traced: 77.1 us -> 70 us
  Pallas kernels: 10.9 us -> 5.85 us
  local copies, waits for them, and re-layouts: 5.71 us -> 2.77 us
  other arithmetic: 4.7 us -> 6.61 us
  starting transfers between devices: 31.6 us -> 30.7 us
    pallas_call x2, Pallas kernels: 10.9 us -> 5.85 us  [attend(): pl.pallas_call(functools.partial(attend_kernel, g, seq_count), out_shape=...]
    unnamed x36 -> x10, local copies, waits for them, and re-layouts: 3.58 us -> 0.02 us
    select_n x2, other arithmetic: 0.13 us -> 1.7 us  [local(): jnp.where(pair ^ k > pair, own[g], prev[g])]
    ppermute x18, starting transfers between devices: 20.8 us -> 19.6 us  [swap(): return lax.ppermute(value, 'seq', [(i, i ^ k) for i in range(seq_count)])]
    another operation x1, other arithmetic: 0.1 us -> 1.06 us  [local(): jnp.stack([lax.dynamic_slice_in_dim(t, (1 - core) * width, width, 1) for...]
    convert_element_type x2, other arithmetic: 1.1 us -> 0.19 us  [local(): prev_sum.astype(jnp.bfloat16)]
  transfers between devices with their start and end apart: 22 -> 22, of which waited for: 5 -> 5; matrix products, arithmetic and copies ran while one was open for 6% -> 9% of each run, Pallas kernels for 14% -> 8%
where the time goes in v1:
time: 68.8 us; the launch traced here: 70 us
  starting transfers between devices  30.7 us (45%)
  waiting for transfers between devices  23.2 us (34%)
  other arithmetic  6.61 us (10%)
  Pallas kernels  5.85 us (9%)
  local copies, waits for them, and re-layouts  2.77 us (4%)
  between operations  0.9 us (1%)
    ppermute x18, starting transfers between devices, swap(): return lax.ppermute(value, 'seq', [(i, i ^ k) for i in range(seq_count)])  19.6 us
    ppermute x2, waiting for transfers between devices, local(): lax.ppermute(prev_sum.astype(jnp.bfloat16), 'dp', [(i + 1, i) for i in ra...  16.5 us
    ppermute x2, starting transfers between devices, local(): lax.ppermute(o, 'dp', [(i, i + 1) for i in range(dp_count - 1)])  8.55 us
    ppermute x18, waiting for transfers between devices, swap(): return lax.ppermute(value, 'seq', [(i, i ^ k) for i in range(seq_count)])  6.65 us
    pallas_call x2, Pallas kernels, attend(): pl.pallas_call(functools.partial(attend_kernel, g, seq_count), out_shape=...  5.85 us
    ppermute x2, starting transfers between devices, local(): lax.ppermute(prev_sum.astype(jnp.bfloat16), 'dp', [(i + 1, i) for i in ra...  2.58 us
    concatenate x3, other arithmetic, join(): return jnp.concatenate(low + high, 1)  2.39 us
    select_n x2, other arithmetic, local(): jnp.where(pair ^ k > pair, own[g], prev[g])  1.7 us
  transfers between devices with their start and end apart: 22, of which 5 were waited for; matrix products, arithmetic and copies ran while one was open for 9% of the time, Pallas kernels for 8%

profile of v1, /device:TPU:0, one launch (start us, length us, event | category | flops | bytes accessed | tf_op | source)
XLA Modules:
  0.0 70.0 jit_solution(5037062680693716871)
XLA Ops:
  0.7 1.6 %constant_dynamic-slice_fusion.6 = (bf16[128,128]{1,0:T(8,128)(2,1)S(1)}, bf16[128,128]{1,0:T(8,128)(2,1)S(1)}, bf16[128,128]{1,0:T(8,128)(2,1)}, bf16[128,128]{...) fusion(bf16[128,512]{1,0:T(8,128)(2,1)} %param.7, ...), kind=kLoop, calls=%fused_computation.67 | loop fusion | bytes 524304 | tf_op jit(solution)/shard_map/dynamic_slice | solution.py:201
  2.9 1.1 %dynamic-slice_bitcast_fusion = (bf16[1,128,2048]{2,1,0:T(8,128)(2,1)S(1)}, bf16[1,128,2048]{2,1,0:T(8,128)(2,1)S(1)}) fusion(bf16[128,4096]{1,0:T(8,128)(2,1)} %o_mine.3, s32[]{:T(128)S(6)} %select_n.166, bf16[128,4096]{1,0:T(8,128)(2,1)S(1)} %copy-done), kind=kLoop, calls=%fused_computation.2 | loop fusion | bytes 2097156 | tf_op jit(solution)/shard_map/stack | solution.py:216
  4.0 1.1 %pad_maximum_fusion = bf16[2,128,2048]{2,1,0:T(8,128)(2,1)} fusion(bf16[1,128,2048]{2,1,0:T(8,128)(2,1)S(1)} %get-tuple-element.59, bf16[1,128,2048]{2,1,0:T(8,128)(2,1)S(1)} %get-tuple-element.60), kind=kLoop, calls=%fused_computation | loop fusion | flops 524288 | bytes 2097152 | tf_op jit(solution)/shard_map/stack | solution.py:216
  5.2 5.1 %collective-permute-start.2 = (bf16[256,256]{1,0:T(8,128)(2,1)S(1)}, bf16[256,256]{1,0:T(8,128)(2,1)S(1)}, u32[]{:S(2)}, u32[]{:S(2)}) collective-permute-start(bf16[256,256]{1,0:T(8,128)(2,1)S(1)} %pad_maximum_fusion.3.refs_0_), channel_id=1, source_target_pairs={{0,8},{8,16},{16,24},{1,9},{9,17},{17,25},{2,10},{10,18},{18,26},{... | collective-permute-start | bytes 393224 | tf_op jit(solution)/shard_map/ppermute | solution.py:212
  11.1 3.5 %collective-permute-start.7 = (bf16[256,256]{1,0:T(8,128)(2,1)S(1)}, bf16[256,256]{1,0:T(8,128)(2,1)S(1)}, u32[]{:S(2)}, u32[]{:S(2)}) collective-permute-start(bf16[256,256]{1,0:T(8,128)(2,1)S(1)} %pad_maximum_fusion.4.refs_0_), channel_id=1, source_target_pairs={{0,8},{8,16},{16,24},{1,9},{9,17},{17,25},{2,10},{10,18},{18,26},{... | collective-permute-start | bytes 393224 | tf_op jit(solution)/shard_map/ppermute | solution.py:212
  15.5 1.6 %collective-permute-start.3 = (bf16[256,256]{1,0:T(8,128)(2,1)S(1)}, bf16[256,256]{1,0:T(8,128)(2,1)S(1)}, u32[]{:S(2)}, u32[]{:S(2)}) collective-permute-start(bf16[256,256]{1,0:T(8,128)(2,1)S(1)} %get-tuple-element.37), channel_id=1, source_target_pairs={{0,2},{1,3},{2,0},{3,1},{4,6},{5,7},{6,4},{7,5},{8,10},{9,11},{10,... | collective-permute-start | bytes 393224 | tf_op jit(solution)/shard_map/ppermute | solution.py:195
  17.0 1.5 %collective-permute-start.4 = (bf16[256,256]{1,0:T(8,128)(2,1)S(1)}, bf16[256,256]{1,0:T(8,128)(2,1)S(1)}, u32[]{:S(2)}, u32[]{:S(2)}) collective-permute-start(bf16[256,256]{1,0:T(8,128)(2,1)S(1)} %get-tuple-element.36), channel_id=1, source_target_pairs={{0,4},{1,5},{2,6},{3,7},{4,0},{5,1},{6,2},{7,3},{8,12},{9,13},{10,... | collective-permute-start | bytes 393224 | tf_op jit(solution)/shard_map/ppermute | solution.py:195
  19.9 2.5 %collective-permute-start.10 = (bf16[256,256]{1,0:T(8,128)(2,1)S(1)}, bf16[256,256]{1,0:T(8,128)(2,1)S(1)}, u32[]{:S(2)}, u32[]{:S(2)}) collective-permute-start(bf16[256,256]{1,0:T(8,128)(2,1)S(1)} %get-tuple-element.38), channel_id=1, source_target_pairs={{0,6},{1,7},{2,4},{3,5},{4,2},{5,3},{6,0},{7,1},{8,14},{9,15},{10,... | collective-permute-start | bytes 393224 | tf_op jit(solution)/shard_map/ppermute | solution.py:195
  23.3 4.0 %collective-permute-done.4.refs_2_ = bf16[256,256]{1,0:T(8,128)(2,1)S(1)} collective-permute-done((bf16[256,256]{1,0:T(8,128)(2,1)S(1)}, bf16[256,256]{1,0:T(8,128)(2,1)S(1)}, u32[]{:S(2)}, u32[]{:S(2)}) %collective-permute-start.4) | collective-permute-done | bytes 131104 | tf_op jit(solution)/shard_map/ppermute | solution.py:195
  27.4 2.4 %collective-permute-start.9 = (bf16[256,256]{1,0:T(8,128)(2,1)S(1)}, bf16[256,256]{1,0:T(8,128)(2,1)S(1)}, u32[]{:S(2)}, u32[]{:S(2)}) collective-permute-start(bf16[256,256]{1,0:T(8,128)(2,1)S(1)} %get-tuple-element.39), channel_id=1, source_target_pairs={{0,4},{1,5},{2,6},{3,7},{4,0},{5,1},{6,2},{7,3},{8,12},{9,13},{10,... | collective-permute-start | bytes 393224 | tf_op jit(solution)/shard_map/ppermute | solution.py:195
  29.8 2.9 %attend_0.1 = (bf16[128,1024]{1,0:T(8,128)(2,1)S(1)}, bf16[128,1024]{1,0:T(8,128)(2,1)S(1)}, f32[256,256]{1,0:T(8,128)S(1)}, bf16[256,256]{1,0:T(8,128)(2,1)S(1)...) custom-call(s32[2]{0:T(128)S(1)} %pad_add_fusion.info_ref, ...), custom_call_target="tpu_custom_call" | custom-call | flops 3355443200 | bytes 8388608 | tf_op jit(solution)/shard_map/attend_0/pallas_call | solution.py:159
  32.7 0.9 %collective-permute-start.12 = (bf16[256,256]{1,0:T(8,128)(2,1)S(1)}, bf16[256,256]{1,0:T(8,128)(2,1)S(1)}, u32[]{:S(2)}, u32[]{:S(2)}) collective-permute-start(bf16[256,256]{1,0:T(8,128)(2,1)S(1)} %get-tuple-element.22), channel_id=1, source_target_pairs={{0,2},{1,3},{2,0},{3,1},{4,6},{5,7},{6,4},{7,5},{8,10},{9,11},{10,... | collective-permute-start | bytes 393224 | tf_op jit(solution)/shard_map/ppermute | solution.py:195
  33.7 1.1 %collective-permute-start.13 = (bf16[256,256]{1,0:T(8,128)(2,1)S(1)}, bf16[256,256]{1,0:T(8,128)(2,1)S(1)}, u32[]{:S(2)}, u32[]{:S(2)}) collective-permute-start(bf16[256,256]{1,0:T(8,128)(2,1)S(1)} %get-tuple-element.23), channel_id=1, source_target_pairs={{0,4},{1,5},{2,6},{3,7},{4,0},{5,1},{6,2},{7,3},{8,12},{9,13},{10,... | collective-permute-start | bytes 393224 | tf_op jit(solution)/shard_map/ppermute | solution.py:195
  34.8 1.5 %collective-permute-start.14 = (bf16[256,256]{1,0:T(8,128)(2,1)S(1)}, bf16[256,256]{1,0:T(8,128)(2,1)S(1)}, u32[]{:S(2)}, u32[]{:S(2)}) collective-permute-start(bf16[256,256]{1,0:T(8,128)(2,1)S(1)} %get-tuple-element.24), channel_id=1, source_target_pairs={{0,6},{1,7},{2,4},{3,5},{4,2},{5,3},{6,0},{7,1},{8,14},{9,15},{10,... | collective-permute-start | bytes 393224 | tf_op jit(solution)/shard_map/ppermute | solution.py:195
  36.3 2.9 %attend_1.1 = (bf16[128,1024]{1,0:T(8,128)(2,1)S(1)}, bf16[128,1024]{1,0:T(8,128)(2,1)S(1)}, f32[256,256]{1,0:T(8,128)S(1)}, bf16[256,256]{1,0:T(8,128)(2,1)S(1)...) custom-call(s32[2]{0:T(128)S(1)} %pad_add_fusion.info_ref, ...), custom_call_target="tpu_custom_call" | custom-call | flops 3355443200 | bytes 8388608 | tf_op jit(solution)/shard_map/attend_1/pallas_call | solution.py:159
  39.2 2.9 %collective-permute-start.17 = (bf16[256,256]{1,0:T(8,128)(2,1)S(1)}, bf16[256,256]{1,0:T(8,128)(2,1)S(1)}, u32[]{:S(2)}, u32[]{:S(2)}) collective-permute-start(bf16[256,256]{1,0:T(8,128)(2,1)S(1)} %get-tuple-element.27), channel_id=1, source_target_pairs={{0,2},{1,3},{2,0},{3,1},{4,6},{5,7},{6,4},{7,5},{8,10},{9,11},{10,... | collective-permute-start | bytes 393224 | tf_op jit(solution)/shard_map/ppermute | solution.py:195
  42.1 1.1 %collective-permute-start.18 = (bf16[256,256]{1,0:T(8,128)(2,1)S(1)}, bf16[256,256]{1,0:T(8,128)(2,1)S(1)}, u32[]{:S(2)}, u32[]{:S(2)}) collective-permute-start(bf16[256,256]{1,0:T(8,128)(2,1)S(1)} %get-tuple-element.28), channel_id=1, source_target_pairs={{0,4},{1,5},{2,6},{3,7},{4,0},{5,1},{6,2},{7,3},{8,12},{9,13},{10,... | collective-permute-start | bytes 393224 | tf_op jit(solution)/shard_map/ppermute | solution.py:195
  43.2 1.4 %collective-permute-start.19 = (bf16[256,256]{1,0:T(8,128)(2,1)S(1)}, bf16[256,256]{1,0:T(8,128)(2,1)S(1)}, u32[]{:S(2)}, u32[]{:S(2)}) collective-permute-start(bf16[256,256]{1,0:T(8,128)(2,1)S(1)} %get-tuple-element.29), channel_id=1, source_target_pairs={{0,6},{1,7},{2,4},{3,5},{4,2},{5,3},{6,0},{7,1},{8,14},{9,15},{10,... | collective-permute-start | bytes 393224 | tf_op jit(solution)/shard_map/ppermute | solution.py:195
  45.2 1.3 %collective-permute-start.15 = (bf16[256,256]{1,0:T(8,128)(2,1)S(1)}, bf16[256,256]{1,0:T(8,128)(2,1)S(1)}, u32[]{:S(2)}, u32[]{:S(2)}) collective-permute-start(bf16[256,256]{1,0:T(8,128)(2,1)S(1)} %fusion.8), channel_id=1, source_target_pairs={{8,0},{16,8},{24,16},{9,1},{17,9},{25,17},{10,2},{18,10},{26,18},{... | collective-permute-start | bytes 393224 | tf_op jit(solution)/shard_map/ppermute | solution.py:239
  47.1 2.0 %collective-permute-done.19 = bf16[256,256]{1,0:T(8,128)(2,1)S(1)} collective-permute-done((bf16[256,256]{1,0:T(8,128)(2,1)S(1)}, bf16[256,256]{1,0:T(8,128)(2,1)S(1)}, u32[]{:S(2)}, u32[]{:S(2)}) %collective-permute-start.19) | collective-permute-done | bytes 131104 | tf_op jit(solution)/shard_map/ppermute | solution.py:195
  49.2 1.3 %collective-permute-start.20 = (bf16[256,256]{1,0:T(8,128)(2,1)S(1)}, bf16[256,256]{1,0:T(8,128)(2,1)S(1)}, u32[]{:S(2)}, u32[]{:S(2)}) collective-permute-start(bf16[256,256]{1,0:T(8,128)(2,1)S(1)} %fusion.17), channel_id=1, source_target_pairs={{8,0},{16,8},{24,16},{9,1},{17,9},{25,17},{10,2},{18,10},{26,18},{... | collective-permute-start | bytes 393224 | tf_op jit(solution)/shard_map/ppermute | solution.py:239
  50.5 14.1 %collective-permute-done.15 = bf16[256,256]{1,0:T(8,128)(2,1)S(1)} collective-permute-done((bf16[256,256]{1,0:T(8,128)(2,1)S(1)}, bf16[256,256]{1,0:T(8,128)(2,1)S(1)}, u32[]{:S(2)}, u32[]{:S(2)}) %collective-permute-start.15) | collective-permute-done | bytes 131104 | tf_op jit(solution)/shard_map/ppermute | solution.py:239
  64.8 2.4 %collective-permute-done.20 = bf16[256,256]{1,0:T(8,128)(2,1)S(1)} collective-permute-done((bf16[256,256]{1,0:T(8,128)(2,1)S(1)}, bf16[256,256]{1,0:T(8,128)(2,1)S(1)}, u32[]{:S(2)}, u32[]{:S(2)}) %collective-permute-start.20) | collective-permute-done | bytes 131104 | tf_op jit(solution)/shard_map/ppermute | solution.py:239
  67.6 1.0 %pad_maximum_fusion.1 = bf16[128,4096]{1,0:T(8,128)(2,1)} fusion(bf16[128,1024]{1,0:T(8,128)(2,1)S(1)} %get-tuple-element.34, bf16[128,1024]{1,0:T(8,128)(2,1)S(1)} %get-tuple-element.32, bf16[128,1024]{1,0:T(8,128)(2,1)S(1)} %get-tuple-element.33, bf16[128,1024]{1,0:T(8,128)(2,1)S(1)} %get-tuple-element.31), kind=kLoop, calls=%fused_computation.1 | loop fusion | flops 4194304 | bytes 2097152 | tf_op jit(solution)/shard_map/concatenate | solution.py:249
  (57 shorter events, 7.8 us)
Async XLA Ops:
  2.3 2.8 %collective-permute-start.1 = (bf16[2,128,256]{2,1,0:T(8,128)(2,1)S(1)}, bf16[2,128,256]{2,1,0:T(8,128)(2,1)S(1)}, u32[]{:S(2)}, u32[]{:S(2)}) collective-permute-start(bf16[2,128,256]{2,1,0:T(8,128)(2,1)S(1)} %pad_maximum_fusion.2), channel_id=1, source_target_pairs={{0,1},{1,0},{2,3},{3,2},{4,5},{5,4},{6,7},{7,6},{8,9},{9,8},{10,11... | collective-permute-start | bytes 393224 | tf_op jit(solution)/shard_map/ppermute | solution.py:195
  5.0 24.7 %collective-permute-start = (bf16[2,128,2048]{2,1,0:T(8,128)(2,1)}, bf16[2,128,2048]{2,1,0:T(8,128)(2,1)S(1)}, u32[]{:S(2)}, u32[]{:S(2)}) collective-permute-start(bf16[2,128,2048]{2,1,0:T(8,128)(2,1)} %pad_maximum_fusion), channel_id=1, source_target_pairs={{0,1},{1,0},{2,3},{3,2},{4,5},{5,4},{6,7},{7,6},{8,9},{9,8},{10,11... | collective-permute-start | bytes 3145736 | tf_op jit(solution)/shard_map/ppermute | solution.py:195
  5.1 24.7 %copy-start.1 = (bf16[128,4096]{1,0:T(8,128)(2,1)S(1)}, bf16[128,4096]{1,0:T(8,128)(2,1)}, u32[]{:S(2)}) copy-start(bf16[128,4096]{1,0:T(8,128)(2,1)} %o_mine.3) | copy-start | bytes 3145732
  5.1 24.7 %copy-start.2 = (s32[16]{0:T(128)S(1)}, s32[16]{0:T(128)}, u32[]{:S(2)}) copy-start(s32[16]{0:T(128)} %doc_ref.3) | copy-start | bytes 196
  5.2 9.4 %collective-permute-start.2 = (bf16[256,256]{1,0:T(8,128)(2,1)S(1)}, bf16[256,256]{1,0:T(8,128)(2,1)S(1)}, u32[]{:S(2)}, u32[]{:S(2)}) collective-permute-start(bf16[256,256]{1,0:T(8,128)(2,1)S(1)} %pad_maximum_fusion.3.refs_0_), channel_id=1, source_target_pairs={{0,8},{8,16},{16,24},{1,9},{9,17},{17,25},{2,10},{10,18},{18,26},{... | collective-permute-start | bytes 393224 | tf_op jit(solution)/shard_map/ppermute | solution.py:212
  11.1 7.9 %collective-permute-start.7 = (bf16[256,256]{1,0:T(8,128)(2,1)S(1)}, bf16[256,256]{1,0:T(8,128)(2,1)S(1)}, u32[]{:S(2)}, u32[]{:S(2)}) collective-permute-start(bf16[256,256]{1,0:T(8,128)(2,1)S(1)} %pad_maximum_fusion.4.refs_0_), channel_id=1, source_target_pairs={{0,8},{8,16},{16,24},{1,9},{9,17},{17,25},{2,10},{10,18},{18,26},{... | collective-permute-start | bytes 393224 | tf_op jit(solution)/shard_map/ppermute | solution.py:212
  15.5 6.9 %collective-permute-start.3 = (bf16[256,256]{1,0:T(8,128)(2,1)S(1)}, bf16[256,256]{1,0:T(8,128)(2,1)S(1)}, u32[]{:S(2)}, u32[]{:S(2)}) collective-permute-start(bf16[256,256]{1,0:T(8,128)(2,1)S(1)} %get-tuple-element.37), channel_id=1, source_target_pairs={{0,2},{1,3},{2,0},{3,1},{4,6},{5,7},{6,4},{7,5},{8,10},{9,11},{10,... | collective-permute-start | bytes 393224 | tf_op jit(solution)/shard_map/ppermute | solution.py:195
  17.0 10.3 %collective-permute-start.4 = (bf16[256,256]{1,0:T(8,128)(2,1)S(1)}, bf16[256,256]{1,0:T(8,128)(2,1)S(1)}, u32[]{:S(2)}, u32[]{:S(2)}) collective-permute-start(bf16[256,256]{1,0:T(8,128)(2,1)S(1)} %get-tuple-element.36), channel_id=1, source_target_pairs={{0,4},{1,5},{2,6},{3,7},{4,0},{5,1},{6,2},{7,3},{8,12},{9,13},{10,... | collective-permute-start | bytes 393224 | tf_op jit(solution)/shard_map/ppermute | solution.py:195
  18.5 11.2 %collective-permute-start.5 = (bf16[256,256]{1,0:T(8,128)(2,1)S(1)}, bf16[256,256]{1,0:T(8,128)(2,1)S(1)}, u32[]{:S(2)}, u32[]{:S(2)}) collective-permute-start(bf16[256,256]{1,0:T(8,128)(2,1)S(1)} %get-tuple-element.35), channel_id=1, source_target_pairs={{0,6},{1,7},{2,4},{3,5},{4,2},{5,3},{6,0},{7,1},{8,14},{9,15},{10,... | collective-permute-start | bytes 393224 | tf_op jit(solution)/shard_map/ppermute | solution.py:195
  19.9 14.9 %collective-permute-start.10 = (bf16[256,256]{1,0:T(8,128)(2,1)S(1)}, bf16[256,256]{1,0:T(8,128)(2,1)S(1)}, u32[]{:S(2)}, u32[]{:S(2)}) collective-permute-start(bf16[256,256]{1,0:T(8,128)(2,1)S(1)} %get-tuple-element.38), channel_id=1, source_target_pairs={{0,6},{1,7},{2,4},{3,5},{4,2},{5,3},{6,0},{7,1},{8,14},{9,15},{10,... | collective-permute-start | bytes 393224 | tf_op jit(solution)/shard_map/ppermute | solution.py:195
  22.4 13.9 %collective-permute-start.8 = (bf16[256,256]{1,0:T(8,128)(2,1)S(1)}, bf16[256,256]{1,0:T(8,128)(2,1)S(1)}, u32[]{:S(2)}, u32[]{:S(2)}) collective-permute-start(bf16[256,256]{1,0:T(8,128)(2,1)S(1)} %get-tuple-element.40), channel_id=1, source_target_pairs={{0,2},{1,3},{2,0},{3,1},{4,6},{5,7},{6,4},{7,5},{8,10},{9,11},{10,... | collective-permute-start | bytes 393224 | tf_op jit(solution)/shard_map/ppermute | solution.py:195
  27.4 8.9 %collective-permute-start.9 = (bf16[256,256]{1,0:T(8,128)(2,1)S(1)}, bf16[256,256]{1,0:T(8,128)(2,1)S(1)}, u32[]{:S(2)}, u32[]{:S(2)}) collective-permute-start(bf16[256,256]{1,0:T(8,128)(2,1)S(1)} %get-tuple-element.39), channel_id=1, source_target_pairs={{0,4},{1,5},{2,6},{3,7},{4,0},{5,1},{6,2},{7,3},{8,12},{9,13},{10,... | collective-permute-start | bytes 393224 | tf_op jit(solution)/shard_map/ppermute | solution.py:195
  32.7 10.5 %collective-permute-start.12 = (bf16[256,256]{1,0:T(8,128)(2,1)S(1)}, bf16[256,256]{1,0:T(8,128)(2,1)S(1)}, u32[]{:S(2)}, u32[]{:S(2)}) collective-permute-start(bf16[256,256]{1,0:T(8,128)(2,1)S(1)} %get-tuple-element.22), channel_id=1, source_target_pairs={{0,2},{1,3},{2,0},{3,1},{4,6},{5,7},{6,4},{7,5},{8,10},{9,11},{10,... | collective-permute-start | bytes 393224 | tf_op jit(solution)/shard_map/ppermute | solution.py:195
  33.7 11.0 %collective-permute-start.13 = (bf16[256,256]{1,0:T(8,128)(2,1)S(1)}, bf16[256,256]{1,0:T(8,128)(2,1)S(1)}, u32[]{:S(2)}, u32[]{:S(2)}) collective-permute-start(bf16[256,256]{1,0:T(8,128)(2,1)S(1)} %get-tuple-element.23), channel_id=1, source_target_pairs={{0,4},{1,5},{2,6},{3,7},{4,0},{5,1},{6,2},{7,3},{8,12},{9,13},{10,... | collective-permute-start | bytes 393224 | tf_op jit(solution)/shard_map/ppermute | solution.py:195
  34.8 9.8 %collective-permute-start.14 = (bf16[256,256]{1,0:T(8,128)(2,1)S(1)}, bf16[256,256]{1,0:T(8,128)(2,1)S(1)}, u32[]{:S(2)}, u32[]{:S(2)}) collective-permute-start(bf16[256,256]{1,0:T(8,128)(2,1)S(1)} %get-tuple-element.24), channel_id=1, source_target_pairs={{0,6},{1,7},{2,4},{3,5},{4,2},{5,3},{6,0},{7,1},{8,14},{9,15},{10,... | collective-permute-start | bytes 393224 | tf_op jit(solution)/shard_map/ppermute | solution.py:195
  39.2 6.0 %collective-permute-start.17 = (bf16[256,256]{1,0:T(8,128)(2,1)S(1)}, bf16[256,256]{1,0:T(8,128)(2,1)S(1)}, u32[]{:S(2)}, u32[]{:S(2)}) collective-permute-start(bf16[256,256]{1,0:T(8,128)(2,1)S(1)} %get-tuple-element.27), channel_id=1, source_target_pairs={{0,2},{1,3},{2,0},{3,1},{4,6},{5,7},{6,4},{7,5},{8,10},{9,11},{10,... | collective-permute-start | bytes 393224 | tf_op jit(solution)/shard_map/ppermute | solution.py:195
  42.1 5.0 %collective-permute-start.18 = (bf16[256,256]{1,0:T(8,128)(2,1)S(1)}, bf16[256,256]{1,0:T(8,128)(2,1)S(1)}, u32[]{:S(2)}, u32[]{:S(2)}) collective-permute-start(bf16[256,256]{1,0:T(8,128)(2,1)S(1)} %get-tuple-element.28), channel_id=1, source_target_pairs={{0,4},{1,5},{2,6},{3,7},{4,0},{5,1},{6,2},{7,3},{8,12},{9,13},{10,... | collective-permute-start | bytes 393224 | tf_op jit(solution)/shard_map/ppermute | solution.py:195
  43.2 5.9 %collective-permute-start.19 = (bf16[256,256]{1,0:T(8,128)(2,1)S(1)}, bf16[256,256]{1,0:T(8,128)(2,1)S(1)}, u32[]{:S(2)}, u32[]{:S(2)}) collective-permute-start(bf16[256,256]{1,0:T(8,128)(2,1)S(1)} %get-tuple-element.29), channel_id=1, source_target_pairs={{0,6},{1,7},{2,4},{3,5},{4,2},{5,3},{6,0},{7,1},{8,14},{9,15},{10,... | collective-permute-start | bytes 393224 | tf_op jit(solution)/shard_map/ppermute | solution.py:195
  44.6 22.8 %collective-permute-start.6 = (bf16[128,1024]{1,0:T(8,128)(2,1)S(1)}, bf16[128,1024]{1,0:T(8,128)(2,1)S(1)}, u32[]{:S(2)}, u32[]{:S(2)}) collective-permute-start(bf16[128,1024]{1,0:T(8,128)(2,1)S(1)} %get-tuple-element.18), channel_id=1, source_target_pairs={{0,1},{1,0},{2,3},{3,2},{4,5},{5,4},{6,7},{7,6},{8,9},{9,8},{10,11... | collective-permute-start | bytes 786440 | tf_op jit(solution)/shard_map/ppermute | solution.py:195
  44.6 22.9 %collective-permute-start.11 = (bf16[128,1024]{1,0:T(8,128)(2,1)S(1)}, bf16[128,1024]{1,0:T(8,128)(2,1)S(1)}, u32[]{:S(2)}, u32[]{:S(2)}) collective-permute-start(bf16[128,1024]{1,0:T(8,128)(2,1)S(1)} %get-tuple-element.20), channel_id=1, source_target_pairs={{0,1},{1,0},{2,3},{3,2},{4,5},{5,4},{6,7},{7,6},{8,9},{9,8},{10,11... | collective-permute-start | bytes 786440 | tf_op jit(solution)/shard_map/ppermute | solution.py:195
  45.2 19.4 %collective-permute-start.15 = (bf16[256,256]{1,0:T(8,128)(2,1)S(1)}, bf16[256,256]{1,0:T(8,128)(2,1)S(1)}, u32[]{:S(2)}, u32[]{:S(2)}) collective-permute-start(bf16[256,256]{1,0:T(8,128)(2,1)S(1)} %fusion.8), channel_id=1, source_target_pairs={{8,0},{16,8},{24,16},{9,1},{17,9},{25,17},{10,2},{18,10},{26,18},{... | collective-permute-start | bytes 393224 | tf_op jit(solution)/shard_map/ppermute | solution.py:239
  49.2 18.0 %collective-permute-start.20 = (bf16[256,256]{1,0:T(8,128)(2,1)S(1)}, bf16[256,256]{1,0:T(8,128)(2,1)S(1)}, u32[]{:S(2)}, u32[]{:S(2)}) collective-permute-start(bf16[256,256]{1,0:T(8,128)(2,1)S(1)} %fusion.17), channel_id=1, source_target_pairs={{8,0},{16,8},{24,16},{9,1},{17,9},{25,17},{10,2},{18,10},{26,18},{... | collective-permute-start | bytes 393224 | tf_op jit(solution)/shard_map/ppermute | solution.py:239
  64.8 3.9 %collective-permute-start.16 = (bf16[128,256]{1,0:T(8,128)(2,1)S(1)}, bf16[128,256]{1,0:T(8,128)(2,1)S(1)}, u32[]{:S(2)}, u32[]{:S(2)}) collective-permute-start(bf16[128,256]{1,0:T(8,128)(2,1)S(1)} %slice.57), channel_id=1, source_target_pairs={{0,1},{1,0},{2,3},{3,2},{4,5},{5,4},{6,7},{7,6},{8,9},{9,8},{10,11... | collective-permute-start | bytes 196616 | tf_op jit(solution)/shard_map/ppermute | solution.py:195
  67.4 1.3 %collective-permute-start.21 = (bf16[128,256]{1,0:T(8,128)(2,1)S(1)}, bf16[128,256]{1,0:T(8,128)(2,1)S(1)}, u32[]{:S(2)}, u32[]{:S(2)}) collective-permute-start(bf16[128,256]{1,0:T(8,128)(2,1)S(1)} %slice.60), channel_id=1, source_target_pairs={{0,1},{1,0},{2,3},{3,2},{4,5},{5,4},{6,7},{7,6},{8,9},{9,8},{10,11... | collective-permute-start | bytes 196616 | tf_op jit(solution)/shard_map/ppermute | solution.py:195
  (3 other events, 7.9 us)

commit v2 on v1

v2 whole, which is shorter than its diff:
```python
import functools

import jax
import jax.numpy as jnp
from jax import lax
from jax.experimental import pallas as pl
from jax.experimental.pallas import tpu as pltpu
from jax.sharding import PartitionSpec as P

QH = 32
KVH = 4
HD = 128
PER_KV = QH // KVH
GROUPS = KVH // 2
MIB = 1024 * 1024
INV_ROOT = HD ** -0.5
TO_LOG2 = INV_ROOT * 1.4426950408889634
NT = (((1,), (1,)), ((), ()))
NN = (((1,), (0,)), ((), ()))
TN = (((0,), (0,)), ((), ()))
K_COLS = pl.ds(0, HD)
V_COLS = pl.ds(HD, HD)


def dot(a, b, dims):
    return lax.dot_general(a, b, dims, preferred_element_type=jnp.float32)


def distance(pair, k, pairs):
    return lax.rem(pair - (pair ^ k) + pairs, pairs)


def place(info_ref, doc_ref, tok, pairs):
    core = lax.rem(info_ref[1], 2)
    chip = info_ref[0] * pairs + info_ref[1] // 2
    first = chip * 2 * tok
    pos = [
        first + (core ^ half) * tok + lax.broadcasted_iota(jnp.int32, (1, tok), 1)
        for half in range(2)
    ]
    starts = [jnp.zeros_like(p) for p in pos]
    low = first * 0
    end = first * 0
    for d in range(doc_ref.shape[0]):
        end = end + doc_ref[d]
        low = jnp.where(first >= end, end, low)
        starts = [jnp.where(p >= end, end, s) for p, s in zip(pos, starts)]
    return core, chip, pos, starts, chip - low // (2 * tok) + 1


def key_rows(core, tok):
    row = lax.broadcasted_iota(jnp.int32, (2 * tok, tok), 0)
    return ((row // tok) ^ core) * tok + lax.rem(row, tok)


def pieces(tok):
    for half in range(2):
        for c in range(PER_KV // 2):
            yield half, pl.ds(c * 2 * tok, 2 * tok), pl.ds((half * PER_KV + 2 * c) * tok, 2 * tok)


def softmax_step(k_tile, v_tile, q_rows, o_rows, bias, peak):
    scores = dot(k_tile, q_rows, NT) * TO_LOG2 + bias
    dprobs = dot(v_tile, o_rows, NT)
    top = jnp.max(scores, 0, keepdims=True)
    new_peak = top if peak is None else jnp.maximum(peak, top)
    weights = jnp.exp2(scores - new_peak)
    total = jnp.sum(weights, 0, keepdims=True)
    mixed = jnp.sum(weights * dprobs, 0, keepdims=True)
    return weights, dprobs, new_peak, total, mixed


def grad_terms(weights, dprobs, peak, stat_ref, cols):
    factor = jnp.exp2(peak - stat_ref[0:1, cols]) * stat_ref[1:2, cols]
    probs = weights * factor
    dscores = probs * (dprobs - stat_ref[2:3, cols])
    return probs.astype(jnp.bfloat16), dscores.astype(jnp.bfloat16)


def own_kernel(pairs, info_ref, doc_ref, *refs):
    blocks = refs[:GROUPS]
    sides = (refs[GROUPS : GROUPS + 2], refs[GROUPS + 2 : GROUPS + 4])
    qo_ref, kept_ref, stat_out, sems = refs[GROUPS + 4 :]
    tok = blocks[0].shape[0] // 2
    width = PER_KV * HD
    core, chip, pos, starts, _ = place(info_ref, doc_ref, tok, pairs)
    key_pos = chip * 2 * tok + key_rows(core, tok)
    biases = []
    for half in range(2):
        bias = jnp.where((key_pos >= starts[half]) & (key_pos <= pos[half]), 0.0, -1e30)
        biases.append(jnp.concatenate([bias, bias], 1))
    mine_at = pl.multiple_of(core * GROUPS * width, HD)
    def slab(g, i, half, h):
        return pltpu.make_async_copy(
            sides[half][i].at[:, pl.ds(pl.multiple_of(mine_at + (g * PER_KV + h) * HD, HD), HD)],
            qo_ref.at[g, i, half, pl.ds(h * tok, tok), :],
            sems.at[g, i, half, h],
        )

    slabs = [
        (g, i, half, h)
        for g in range(GROUPS)
        for half in range(2)
        for h in range(PER_KV)
        for i in range(2)
    ]
    for at in slabs:
        slab(*at).start()
    for g in range(GROUPS):
        k_tile = blocks[g][:, K_COLS]
        v_tile = blocks[g][:, V_COLS]
        for half, rows, cols in pieces(tok):
            if rows.start == 0:
                for at in slabs:
                    if at[0] == g and at[2] == half:
                        slab(*at).wait()
            weights, dprobs, peak, total, mixed = softmax_step(
                k_tile, v_tile, qo_ref[g, 0, half, rows, :], qo_ref[g, 1, half, rows, :], biases[half], None
            )
            kept_ref[g, 0, :, cols] = weights
            kept_ref[g, 1, :, cols] = dprobs
            stat_out[g, 0:1, cols] = peak
            stat_out[g, 1:2, cols] = total
            stat_out[g, 2:3, cols] = mixed


def reach_kernel(g, pairs, info_ref, doc_ref, qo_ref, first_stat, *refs):
    kv_refs = refs[: pairs + 1]
    refs = refs[-(2 * pairs + 3 + 4 - pairs) :]
    part_outs = refs[:pairs]
    ds_out, kv_all, stat_ref, weight_s, dprob_s, peak_s, dkv_s = refs[pairs:]
    keys = kv_refs[0].shape[0]
    tok = keys // 2
    pair = info_ref[1] // 2
    core, chip, _, starts, count = place(info_ref, doc_ref, tok, pairs)

    kv_all[0] = kv_refs[0][...]
    kv_all[pairs] = kv_refs[pairs][...]
    for k in range(1, pairs):
        kv_all[distance(pair, k, pairs)] = kv_refs[k][...]
    dkv_s[...] = jnp.zeros_like(dkv_s)
    stat_ref[...] = first_stat[g]
    row = key_rows(core, tok)

    def stat_step(back, carry):
        k_tile = kv_all[back, :, K_COLS]
        v_tile = kv_all[back, :, V_COLS]
        key_pos = (chip - back) * keys + row
        biases = []
        for half in range(2):
            bias = jnp.where(key_pos >= starts[half], 0.0, -1e30)
            biases.append(jnp.concatenate([bias, bias], 1))
        for half, rows, cols in pieces(tok):
            old = stat_ref[0:1, cols]
            weights, dprobs, peak, total, mixed = softmax_step(
                k_tile, v_tile, qo_ref[g, 0, half, rows, :], qo_ref[g, 1, half, rows, :], biases[half], old
            )
            rescale = jnp.exp2(old - peak)
            stat_ref[0:1, cols] = peak
            stat_ref[1:2, cols] = stat_ref[1:2, cols] * rescale + total
            stat_ref[2:3, cols] = stat_ref[2:3, cols] * rescale + mixed
            weight_s[back - 1, :, cols] = weights
            dprob_s[back - 1, :, cols] = dprobs
            peak_s[back - 1, :, cols] = peak
        return carry

    lax.fori_loop(1, count, stat_step, 0)
    inv_total = 1.0 / stat_ref[1:2, :]
    stat_ref[1:2, :] = inv_total
    stat_ref[2:3, :] = stat_ref[2:3, :] * inv_total

    def grad_step(back, carry):
        dk = jnp.zeros((keys, HD), jnp.float32)
        dv = jnp.zeros((keys, HD), jnp.float32)
        for half, rows, cols in pieces(tok):
            probs_b, dscores = grad_terms(
                weight_s[back - 1, :, cols],
                dprob_s[back - 1, :, cols],
                peak_s[back - 1, :, cols],
                stat_ref,
                cols,
            )
            dv = dv + dot(probs_b, qo_ref[g, 1, half, rows, :], NN)
            dk = dk + dot(dscores, qo_ref[g, 0, half, rows, :], NN)
            ds_out[back - 1, :, cols] = dscores
        dkv_s[back - 1, :, K_COLS] = (dk * INV_ROOT).astype(jnp.bfloat16)
        dkv_s[back - 1, :, V_COLS] = dv.astype(jnp.bfloat16)
        return carry

    lax.fori_loop(1, count, grad_step, 0)
    part_outs[pairs - 1][...] = dkv_s[pairs - 1]
    for k in range(1, pairs):
        part_outs[k - 1][...] = dkv_s[distance(pair, k, pairs) - 1]


def rest_kernel(
    g, pairs, info_ref, doc_ref, qo_ref, kept_ref, first_stat, stat_ref, ds_ref, kv_ref, *refs
):
    own_out, dq_mine, dq_theirs, dq_s = refs[-4:]
    keys = kv_ref.shape[1]
    tok = keys // 2
    count = place(info_ref, doc_ref, tok, pairs)[-1]
    k_tile = kv_ref[0, :, K_COLS]
    dk = jnp.zeros((keys, HD), jnp.float32)
    dv = jnp.zeros((keys, HD), jnp.float32)
    for half, rows, cols in pieces(tok):
        probs_b, dscores = grad_terms(
            kept_ref[g, 0, :, cols], kept_ref[g, 1, :, cols], first_stat[g, 0:1, cols], stat_ref, cols
        )
        dv = dv + dot(probs_b, qo_ref[g, 1, half, rows, :], NN)
        dk = dk + dot(dscores, qo_ref[g, 0, half, rows, :], NN)
        dq_s[:, cols] = dot(k_tile, dscores, TN)
    own_out[:, K_COLS] = dk * INV_ROOT
    own_out[:, V_COLS] = dv

    def query_step(back, carry):
        k_tile = kv_ref[back, :, K_COLS]
        for half, rows, cols in pieces(tok):
            dq_s[:, cols] += dot(k_tile, ds_ref[back - 1, :, cols], TN)
        return carry

    lax.fori_loop(1, count, query_step, 0)
    for half, dq_ref in enumerate((dq_mine, dq_theirs)):
        for h in range(PER_KV):
            block = dq_s[:, pl.ds((half * PER_KV + h) * tok, tok)] * INV_ROOT
            dq_ref[:, pl.ds(h * HD, HD)] = block.T.astype(jnp.bfloat16)


def finish_kernel(tok, info_ref, *refs):
    own = refs[:GROUPS]
    back = refs[GROUPS : 2 * GROUPS]
    own_other = refs[2 * GROUPS]
    back_other = refs[2 * GROUPS + 1 : 3 * GROUPS + 1]
    grad_k, grad_v = refs[3 * GROUPS + 1 :]
    core = lax.rem(info_ref[1], 2)
    for g in range(GROUPS):
        mine = own[g][:tok] + back[g][:tok].astype(jnp.float32)
        other = own_other[g] + back_other[g][tok:].astype(jnp.float32)
        for total, side in ((mine, core), (other, 1 - core)):
            cols = pl.ds(pl.multiple_of((side * GROUPS + g) * HD, HD), HD)
            grad_k[:, cols] = total[:, :HD].astype(jnp.bfloat16)
            grad_v[:, cols] = total[:, HD:].astype(jnp.bfloat16)


def nbytes(shapes):
    total = 0
    for s in shapes:
        size = jnp.dtype(s.dtype).itemsize
        for n in s.shape:
            size *= n
        total += size
    return total


def call(kernel, name, scalars, arrays, out_shape, scratch=(), flops=0, passing=(), hbm=(), sems=None):
    smem = pl.BlockSpec(memory_space=pltpu.SMEM)
    vmem = pl.BlockSpec(memory_space=pltpu.VMEM)
    used = nbytes(arrays) + nbytes(out_shape) + nbytes(scratch)
    return pl.pallas_call(
        kernel,
        out_shape=out_shape,
        in_specs=[smem] * len(scalars)
        + [vmem] * len(arrays)
        + [pl.BlockSpec(memory_space=pl.ANY)] * (len(hbm) + len(passing)),
        out_specs=[vmem] * len(out_shape),
        scratch_shapes=[pltpu.VMEM(s.shape, s.dtype) for s in scratch]
        + ([pltpu.SemaphoreType.DMA(sems)] if sems else []),
        compiler_params=pltpu.CompilerParams(vmem_limit_bytes=used + 3 * MIB),
        cost_estimate=pl.CostEstimate(
            flops=flops, bytes_accessed=nbytes(arrays) + nbytes(out_shape), transcendentals=0
        ),
        name=name,
    )(*scalars, *arrays, *(pltpu.with_memory_space_constraint(a, pltpu.HBM) for a in hbm), *passing)


def local(queries, keys, values, grad_out, doc_lengths):
    tok = queries.shape[0]
    dp_count = lax.axis_size("dp")
    seq_count = lax.axis_size("seq")
    pairs = seq_count // 2
    dp_idx = lax.axis_index("dp")
    seq_idx = lax.axis_index("seq")
    core = lax.rem(seq_idx, 2)
    pair = seq_idx // 2
    rows = 2 * tok
    lanes = 2 * PER_KV * tok
    f32, bf16 = jnp.float32, jnp.bfloat16
    shape = jax.ShapeDtypeStruct

    def swap(value, k):
        return lax.ppermute(value, "seq", [(i, i ^ k) for i in range(seq_count)])

    k_theirs = swap(keys, 1)
    v_theirs = swap(values, 1)

    def block(g):
        at = (core * GROUPS + g) * HD
        cut = [
            [lax.dynamic_slice_in_dim(t, at, HD, 1) for t in side]
            for side in ((keys, values), (k_theirs, v_theirs))
        ]
        return jnp.concatenate([jnp.concatenate(side, 1) for side in cut], 0)

    own = [block(g) for g in range(GROUPS)]
    prev = [lax.ppermute(o, "dp", [(i, (i + 1) % dp_count) for i in range(dp_count)]) for o in own]
    q_sent, o_sent, _ = lax.optimization_barrier((queries, grad_out, own[-1]))
    q_theirs, o_theirs = swap(q_sent, 1), swap(o_sent, 1)
    info = jnp.stack([dp_idx, seq_idx]).astype(jnp.int32)
    scalars = [info, doc_lengths]

    blocks = []
    for g in range(GROUPS):
        own_now, prev_now = own[g], prev[g]
        if g:
            own_now, *_ = lax.optimization_barrier((own_now, *chosen))
        chosen = [jnp.where((pair ^ k) > pair, own_now, prev_now) for k in range(1, pairs)]
        sent = [swap(c, 2 * k) for k, c in enumerate(chosen, 1)]
        blocks.append([own[g]] + sent + [prev[g]])

    stat = shape((3, lanes), f32)
    unit = 2 * rows * lanes * HD
    outs = call(
        functools.partial(own_kernel, pairs),
        "own",
        scalars,
        own,
        [
            shape((GROUPS, 2, 2, PER_KV * tok, HD), bf16),
            shape((GROUPS, 2, rows, lanes), f32),
            shape((GROUPS, 3, lanes), f32),
        ],
        flops=2 * GROUPS * unit,
        hbm=[queries, grad_out, q_theirs, o_theirs],
        sems=(GROUPS, 2, 2, PER_KV),
    )
    qo, kept, first_stats = outs

    part = shape((rows, 2 * HD), bf16)
    reached, own_parts = [], []
    for g in range(GROUPS):
        stats = first_stats
        if g:
            stats, _ = lax.optimization_barrier((stats, reached[-1][pairs + 2]))
        reached.append(
            call(
                functools.partial(reach_kernel, g, pairs),
                "reach_%d" % g,
                scalars,
                [qo, stats] + blocks[g],
                [part] * pairs
                + [shape((pairs, rows, lanes), bf16), shape((pairs + 1, rows, 2 * HD), bf16), stat],
                [
                    shape((pairs, rows, lanes), f32),
                    shape((pairs, rows, lanes), f32),
                    shape((pairs, 1, lanes), f32),
                    shape((pairs, rows, 2 * HD), bf16),
                ],
                flops=4 * pairs * unit,
                passing=[kept] + [r[pairs] for r in reached],
            )
        )
    own_sums, backs, marks = [], [], []
    for g in range(GROUPS):
        prev_sum = reached[g][pairs - 1].astype(f32)
        own_sum = 0.0
        received = [swap(reached[g][k - 1], 2 * k) for k in range(1, pairs)]
        for k in range(1, pairs):
            back = received[k - 1].astype(f32)
            later = (pair ^ k) > pair
            own_sum = own_sum + jnp.where(later, back, 0.0)
            prev_sum = prev_sum + jnp.where(later, 0.0, back)
        own_sums.append(own_sum)
        prev_sum = prev_sum.astype(bf16)
        marks.append(prev_sum)
        backs.append(
            lax.ppermute(
                prev_sum, "dp", [((i + 1) % dp_count, i) for i in range(dp_count)]
            )
        )
    dq_mine, dq_other = [], []
    for g in range(GROUPS):
        ds, kv, stats = reached[g][pairs:]
        stats, _ = lax.optimization_barrier((stats, marks[g]))
        dq_shape = shape((tok, PER_KV * HD), bf16)
        own_part, mine, theirs = call(
            functools.partial(rest_kernel, g, pairs),
            "rest_%d" % g,
            scalars,
            [qo, kept, first_stats, stats, ds, kv],
            [shape((rows, 2 * HD), f32), dq_shape, dq_shape],
            [shape((HD, lanes), f32)],
            flops=(3 + pairs) * unit,
            passing=[r[pairs] for r in reached[g + 1 :]],
        )
        own_sums[g] = own_sums[g] + own_part
        dq_mine.append(mine)
        dq_other.append(swap(theirs, 1))
    own_other = swap(jnp.stack([t[tok:] for t in own_sums]), 1)
    low = [jnp.where(core == 0, x, y) for x, y in zip(dq_mine, dq_other)]
    high = [jnp.where(core == 0, y, x) for x, y in zip(dq_mine, dq_other)]
    grad_q = jnp.concatenate(low + high, 1)
    grad_q, own_other, backs[-1] = lax.optimization_barrier((grad_q, own_other, backs[-1]))
    back_other = [swap(b, 1) for b in backs]
    out = shape((tok, KVH * HD), bf16)
    grad_k, grad_v = call(
        functools.partial(finish_kernel, tok),
        "finish",
        [info],
        own_sums + backs + [own_other] + back_other,
        [out, out],
    )
    return (grad_q, grad_k, grad_v)


def solution(mesh):
    spec = P(("dp", "seq"), None)
    return jax.shard_map(
        local,
        mesh=mesh,
        in_specs=(spec, spec, spec, spec, P()),
        out_specs=(spec, spec, spec),
        check_vma=False,
    )
```

time: 68.8 us -> 60.8 us (0.88); the launches traced: 70 us -> 60.1 us
  waiting for transfers between devices: 23.2 us -> 6.82 us
  starting transfers between devices: 30.7 us -> 39.5 us
  other arithmetic: 6.61 us -> 1.72 us
  Pallas kernels: 5.85 us -> 10.4 us
  local copies, waits for them, and re-layouts: 2.77 us -> 0.87 us
    ppermute x4, waiting for transfers between devices: 16.5 us -> 4.63 us  [the longest x2 4.63 us: local(): lax.ppermute(o, 'dp', [(i, (i + 1) % dp_count) for i in range(dp_count)])]
    ppermute x18 -> x21, starting transfers between devices: 19.6 us -> 26.9 us  [swap(): return lax.ppermute(value, 'seq', [(i, i ^ k) for i in range(seq_count)])]
    pallas_call x2 -> x6, Pallas kernels: 5.85 us -> 10.4 us  [call(): pl.pallas_call(kernel, out_shape=out_shape, in_specs=[smem] * len(scalars...]
    ppermute x18 -> x21, waiting for transfers between devices: 6.65 us -> 2.19 us  [swap(): return lax.ppermute(value, 'seq', [(i, i ^ k) for i in range(seq_count)])]
    concatenate x5 -> x3, other arithmetic: 3.19 us -> 1.08 us  [the longest x1 1.04 us: local(): grad_q = jnp.concatenate(low + high, 1)]
    select_n x6 -> x4, other arithmetic: 1.84 us -> 0.18 us  [the longest x2 0.1 us: local(): jnp.where(pair ^ k > pair, own_now, prev_now)]
    ppermute x4, starting transfers between devices: 11.1 us -> 12.5 us  [the longest x2 8.14 us: local(): lax.ppermute(prev_sum, 'dp', [((i + 1) % dp_count, i) for i in range(dp_c...]
    another operation x1 -> x2, local copies, waits for them, and re-layouts: 1.12 us -> 0.02 us  [local(): own_other = swap(jnp.stack([t[tok:] for t in own_sums]), 1)]
  transfers between devices with their start and end apart: 22 -> 25, of which waited for: 5 -> 5; matrix products, arithmetic and copies ran while one was open for 9% -> 4% of each run, Pallas kernels for 8% -> 15%
where the time goes in v2:
time: 60.8 us; the launch traced here: 60.1 us
  starting transfers between devices  39.5 us (65%)
  Pallas kernels  10.4 us (17%)
  waiting for transfers between devices  6.82 us (11%)
  other arithmetic  1.72 us (3%)
  local copies, waits for them, and re-layouts  0.87 us (1%)
  between operations  0.83 us (1%)
    ppermute x21, starting transfers between devices, swap(): return lax.ppermute(value, 'seq', [(i, i ^ k) for i in range(seq_count)])  26.9 us
    pallas_call x6, Pallas kernels, call(): pl.pallas_call(kernel, out_shape=out_shape, in_specs=[smem] * len(scalars...  10.4 us
    ppermute x2, starting transfers between devices, local(): lax.ppermute(prev_sum, 'dp', [((i + 1) % dp_count, i) for i in range(dp_c...  8.14 us
    ppermute x2, waiting for transfers between devices, local(): lax.ppermute(o, 'dp', [(i, (i + 1) % dp_count) for i in range(dp_count)])  4.63 us
    ppermute x2, starting transfers between devices, local(): lax.ppermute(o, 'dp', [(i, (i + 1) % dp_count) for i in range(dp_count)])  4.39 us
    ppermute x21, waiting for transfers between devices, swap(): return lax.ppermute(value, 'seq', [(i, i ^ k) for i in range(seq_count)])  2.19 us
  transfers between devices with their start and end apart: 25, of which 5 were waited for; matrix products, arithmetic and copies ran while one was open for 4% of the time, Pallas kernels for 15%

profile of v2, /device:TPU:0, one launch (start us, length us, event | category | flops | bytes accessed | tf_op | source)
XLA Modules:
  0.0 60.1 jit_solution(1712216056543475844)
XLA Ops:
  1.2 0.8 %constant_dynamic-slice_fusion.2 = (bf16[128,128]{1,0:T(8,128)(2,1)S(1)}, bf16[128,128]{1,0:T(8,128)(2,1)S(1)}, bf16[128,128]{1,0:T(8,128)(2,1)S(1)}, bf16[128,128]{1,0:T(8,128)(2,1)S(1)}) fusion(bf16[128,512]{1,0:T(8,128)(2,1)} %param.7, s32[]{:T(128)S(6)} %select_n.123, s32[]{:T(128)S(6)} %select_n.122, bf16[128,512]{1,0:T(8,128)(2,1)} %param.6), kind=kLoop, calls=%fused_computation.44 | loop fusion | bytes 262152 | tf_op jit(solution)/shard_map/dynamic_slice | solution.py:299
  3.4 2.8 %collective-permute-start.4 = (bf16[256,256]{1,0:T(8,128)(2,1)S(1)}, bf16[256,256]{1,0:T(8,128)(2,1)S(1)}, u32[]{:S(2)}, u32[]{:S(2)}) collective-permute-start(bf16[256,256]{1,0:T(8,128)(2,1)S(1)} %maximum_maximum_fusion.refs_0_), channel_id=1, source_target_pairs={{0,8},{8,16},{16,24},{24,0},{1,9},{9,17},{17,25},{25,1},{2,10},{10... | collective-permute-start | bytes 393224 | tf_op jit(solution)/shard_map/ppermute | solution.py:305
  6.2 1.6 %collective-permute-start.11 = (bf16[256,256]{1,0:T(8,128)(2,1)S(1)}, bf16[256,256]{1,0:T(8,128)(2,1)S(1)}, u32[]{:S(2)}, u32[]{:S(2)}) collective-permute-start(bf16[256,256]{1,0:T(8,128)(2,1)S(1)} %maximum_maximum_fusion.1.refs_1_.refs_0_), channel_id=1, source_target_pairs={{0,8},{8,16},{16,24},{24,0},{1,9},{9,17},{17,25},{25,1},{2,10},{10... | collective-permute-start | bytes 393224 | tf_op jit(solution)/shard_map/ppermute | solution.py:305
  7.8 4.6 %collective-permute-done.4.refs_4_ = bf16[256,256]{1,0:T(8,128)(2,1)S(1)} collective-permute-done((bf16[256,256]{1,0:T(8,128)(2,1)S(1)}, bf16[256,256]{1,0:T(8,128)(2,1)S(1)}, u32[]{:S(2)}, u32[]{:S(2)}) %collective-permute-start.4) | collective-permute-done | bytes 131104 | tf_op jit(solution)/shard_map/ppermute | solution.py:305
  12.5 1.8 %collective-permute-start.5 = (bf16[256,256]{1,0:T(8,128)(2,1)S(1)}, bf16[256,256]{1,0:T(8,128)(2,1)S(1)}, u32[]{:S(2)}, u32[]{:S(2)}) collective-permute-start(bf16[256,256]{1,0:T(8,128)(2,1)S(1)} %get-tuple-element.80), channel_id=1, source_target_pairs={{0,2},{1,3},{2,0},{3,1},{4,6},{5,7},{6,4},{7,5},{8,10},{9,11},{10,... | collective-permute-start | bytes 393224 | tf_op jit(solution)/shard_map/ppermute | solution.py:291
  14.3 1.5 %collective-permute-start.6 = (bf16[256,256]{1,0:T(8,128)(2,1)S(1)}, bf16[256,256]{1,0:T(8,128)(2,1)S(1)}, u32[]{:S(2)}, u32[]{:S(2)}) collective-permute-start(bf16[256,256]{1,0:T(8,128)(2,1)S(1)} %get-tuple-element.79), channel_id=1, source_target_pairs={{0,4},{1,5},{2,6},{3,7},{4,0},{5,1},{6,2},{7,3},{8,12},{9,13},{10,... | collective-permute-start | bytes 393224 | tf_op jit(solution)/shard_map/ppermute | solution.py:291
  15.8 1.6 %collective-permute-start.7 = (bf16[256,256]{1,0:T(8,128)(2,1)S(1)}, bf16[256,256]{1,0:T(8,128)(2,1)S(1)}, u32[]{:S(2)}, u32[]{:S(2)}) collective-permute-start(bf16[256,256]{1,0:T(8,128)(2,1)S(1)} %get-tuple-element.78), channel_id=1, source_target_pairs={{0,6},{1,7},{2,4},{3,5},{4,2},{5,3},{6,0},{7,1},{8,14},{9,15},{10,... | collective-permute-start | bytes 393224 | tf_op jit(solution)/shard_map/ppermute | solution.py:291
  17.5 0.6 collective-permute-start.12
  18.1 1.4 %collective-permute-start.13 = (bf16[256,256]{1,0:T(8,128)(2,1)S(1)}, bf16[256,256]{1,0:T(8,128)(2,1)S(1)}, u32[]{:S(2)}, u32[]{:S(2)}) collective-permute-start(bf16[256,256]{1,0:T(8,128)(2,1)S(1)} %get-tuple-element.76), channel_id=1, source_target_pairs={{0,4},{1,5},{2,6},{3,7},{4,0},{5,1},{6,2},{7,3},{8,12},{9,13},{10,... | collective-permute-start | bytes 393224 | tf_op jit(solution)/shard_map/ppermute | solution.py:291
  19.5 4.4 %own.1 = (bf16[2,2,2,1024,128]{4,3,2,1,0:T(8,128)(2,1)S(1)}, f32[2,2,256,2048]{3,2,1,0:T(8,128)S(1)}, f32[2,3,2048]{2,1,0:T(4,128)S(1)}) custom-call(s32[2]{0:T(128)S(1)} %pad_add_fusion.info_ref, s32[16]{0:T(128)S(1)} %copy-done, bf16[256,256]{1,0:T(8,128)(2,1)S(1)} %maximum_maximum_fusion.refs_0_, ...), custom_call_target="tpu_custom_call" | custom-call | flops 536870912 | bytes 10797056 | tf_op jit(solution)/shard_map/own/pallas_call | solution.py:259
  23.9 1.6 %collective-permute-start.14 = (bf16[256,256]{1,0:T(8,128)(2,1)S(1)}, bf16[256,256]{1,0:T(8,128)(2,1)S(1)}, u32[]{:S(2)}, u32[]{:S(2)}) collective-permute-start(bf16[256,256]{1,0:T(8,128)(2,1)S(1)} %get-tuple-element.75), channel_id=1, source_target_pairs={{0,6},{1,7},{2,4},{3,5},{4,2},{5,3},{6,0},{7,1},{8,14},{9,15},{10,... | collective-permute-start | bytes 393224 | tf_op jit(solution)/shard_map/ppermute | solution.py:291
  25.6 0.7 %reach_0.1 = (bf16[256,256]{1,0:T(8,128)(2,1)S(1)}, bf16[256,256]{1,0:T(8,128)(2,1)S(1)}, bf16[256,256]{1,0:T(8,128)(2,1)S(1)}, bf16[256,256]{1,0:T(8,128)(2,1)S...) custom-call(s32[2]{0:T(128)S(1)} %pad_add_fusion.info_ref, ...), custom_call_target="tpu_custom_call" | custom-call | flops 2147483648 | bytes 8200192 | tf_op jit(solution)/shard_map/reach_0/pallas_call | solution.py:259
  26.3 6.5 %collective-permute-start.10 = (bf16[256,256]{1,0:T(8,128)(2,1)S(1)}, bf16[256,256]{1,0:T(8,128)(2,1)S(1)}, u32[]{:S(2)}, u32[]{:S(2)}) collective-permute-start(bf16[256,256]{1,0:T(8,128)(2,1)S(1)} %get-tuple-element.46), channel_id=1, source_target_pairs={{0,6},{1,7},{2,4},{3,5},{4,2},{5,3},{6,0},{7,1},{8,14},{9,15},{10,... | collective-permute-start | bytes 393224 | tf_op jit(solution)/shard_map/ppermute | solution.py:291
  32.8 0.6 %collective-permute-start.9 = (bf16[256,256]{1,0:T(8,128)(2,1)S(1)}, bf16[256,256]{1,0:T(8,128)(2,1)S(1)}, u32[]{:S(2)}, u32[]{:S(2)}) collective-permute-start(bf16[256,256]{1,0:T(8,128)(2,1)S(1)} %get-tuple-element.45), channel_id=1, source_target_pairs={{0,4},{1,5},{2,6},{3,7},{4,0},{5,1},{6,2},{7,3},{8,12},{9,13},{10,... | collective-permute-start | bytes 393224 | tf_op jit(solution)/shard_map/ppermute | solution.py:291
  33.4 0.7 %reach_1.1 = (bf16[256,256]{1,0:T(8,128)(2,1)S(1)}, bf16[256,256]{1,0:T(8,128)(2,1)S(1)}, bf16[256,256]{1,0:T(8,128)(2,1)S(1)}, bf16[256,256]{1,0:T(8,128)(2,1)S...) custom-call(s32[2]{0:T(128)S(1)} %pad_add_fusion.info_ref, ...), custom_call_target="tpu_custom_call" | custom-call | flops 2147483648 | bytes 8200192 | tf_op jit(solution)/shard_map/reach_1/pallas_call | solution.py:259
  34.2 3.2 %collective-permute-start.16 = (bf16[256,256]{1,0:T(8,128)(2,1)S(1)}, bf16[256,256]{1,0:T(8,128)(2,1)S(1)}, u32[]{:S(2)}, u32[]{:S(2)}) collective-permute-start(bf16[256,256]{1,0:T(8,128)(2,1)S(1)} %get-tuple-element.57), channel_id=1, source_target_pairs={{0,2},{1,3},{2,0},{3,1},{4,6},{5,7},{6,4},{7,5},{8,10},{9,11},{10,... | collective-permute-start | bytes 393224 | tf_op jit(solution)/shard_map/ppermute | solution.py:291
  37.3 5.4 %collective-permute-start.17 = (bf16[256,256]{1,0:T(8,128)(2,1)S(1)}, bf16[256,256]{1,0:T(8,128)(2,1)S(1)}, u32[]{:S(2)}, u32[]{:S(2)}) collective-permute-start(bf16[256,256]{1,0:T(8,128)(2,1)S(1)} %get-tuple-element.58), channel_id=1, source_target_pairs={{0,4},{1,5},{2,6},{3,7},{4,0},{5,1},{6,2},{7,3},{8,12},{9,13},{10,... | collective-permute-start | bytes 393224 | tf_op jit(solution)/shard_map/ppermute | solution.py:291
  42.9 6.7 %collective-permute-start.22 = (bf16[256,256]{1,0:T(8,128)(2,1)S(1)}, bf16[256,256]{1,0:T(8,128)(2,1)S(1)}, u32[]{:S(2)}, u32[]{:S(2)}) collective-permute-start(bf16[256,256]{1,0:T(8,128)(2,1)S(1)} %fusion.3), channel_id=1, source_target_pairs={{8,0},{16,8},{24,16},{0,24},{9,1},{17,9},{25,17},{1,25},{10,2},{18... | collective-permute-start | bytes 393224 | tf_op jit(solution)/shard_map/ppermute | solution.py:376
  49.6 1.6 %rest_0.1 = (f32[256,256]{1,0:T(8,128)S(1)}, bf16[128,1024]{1,0:T(8,128)(2,1)S(1)}, bf16[128,1024]{1,0:T(8,128)(2,1)S(1)}) custom-call(s32[2]{0:T(128)S(1)} %pad_add_fusion.info_ref, s32[16]{0:T(128)S(1)} %copy-done, bf16[2,2,2,1024,128]{4,3,2,1,0:T(8,128)(2,1)S(1)} %get-tuple-element.39.qo_ref, f32[2,2,256,2048]{3,2,1,0:T(8,128)S(1)} %get-tuple-element.40.refs_5_.kept_ref, ...), custom_call_target="tpu_custom_call" | custom-call | flops 939524096 | bytes 16195584 | tf_op jit(solution)/shard_map/rest_0/pallas_call | solution.py:259
  51.5 1.4 %collective-permute-start.21 = (bf16[256,256]{1,0:T(8,128)(2,1)S(1)}, bf16[256,256]{1,0:T(8,128)(2,1)S(1)}, u32[]{:S(2)}, u32[]{:S(2)}) collective-permute-start(bf16[256,256]{1,0:T(8,128)(2,1)S(1)} %fusion.10), channel_id=1, source_target_pairs={{8,0},{16,8},{24,16},{0,24},{9,1},{17,9},{25,17},{1,25},{10,2},{18... | collective-permute-start | bytes 393224 | tf_op jit(solution)/shard_map/ppermute | solution.py:376
  52.9 1.6 %rest_1.1 = (f32[256,256]{1,0:T(8,128)S(1)}, bf16[128,1024]{1,0:T(8,128)(2,1)S(1)}, bf16[128,1024]{1,0:T(8,128)(2,1)S(1)}) custom-call(s32[2]{0:T(128)S(1)} %pad_add_fusion.info_ref, s32[16]{0:T(128)S(1)} %copy-done, bf16[2,2,2,1024,128]{4,3,2,1,0:T(8,128)(2,1)S(1)} %get-tuple-element.39.qo_ref, f32[2,2,256,2048]{3,2,1,0:T(8,128)S(1)} %get-tuple-element.40.refs_5_.kept_ref, ...), custom_call_target="tpu_custom_call" | custom-call | flops 939524096 | bytes 16195584 | tf_op jit(solution)/shard_map/rest_1/pallas_call | solution.py:259
  56.4 1.0 %pad_maximum_fusion = bf16[128,4096]{1,0:T(8,128)(2,1)} fusion(bf16[128,1024]{1,0:T(8,128)(2,1)S(1)} %get-tuple-element.74, bf16[128,1024]{1,0:T(8,128)(2,1)S(1)} %get-tuple-element.72, bf16[128,1024]{1,0:T(8,128)(2,1)S(1)} %get-tuple-element.73, bf16[128,1024]{1,0:T(8,128)(2,1)S(1)} %get-tuple-element.71), kind=kLoop, calls=%fused_computation | loop fusion | flops 4194304 | bytes 2097152 | tf_op jit(solution)/shard_map/concatenate | solution.py:401
  57.8 1.0 %collective-permute-done.24.refs_6_ = bf16[256,256]{1,0:T(8,128)(2,1)S(1)} collective-permute-done((bf16[256,256]{1,0:T(8,128)(2,1)S(1)}, bf16[256,256]{1,0:T(8,128)(2,1)S(1)}, u32[]{:S(2)}, u32[]{:S(2)}) %collective-permute-start.24) | collective-permute-done | bytes 131104 | tf_op jit(solution)/shard_map/ppermute | solution.py:291
  58.8 1.3 %finish.1 = (bf16[128,512]{1,0:T(8,128)(2,1)}, bf16[128,512]{1,0:T(8,128)(2,1)}) custom-call(s32[2]{0:T(128)S(1)} %pad_add_fusion.info_ref, f32[256,256]{1,0:T(8,128)S(1)} %fusion.6.refs_0_, f32[256,256]{1,0:T(8,128)S(1)} %fusion.13.refs_1_, bf16[256,256]{1,0:T(8,128)(2,1)S(1)} %collective-permute-done.22.refs_2_, ...), custom_call_target="tpu_custom_call" | custom-call | bytes 1572864 | tf_op jit(solution)/shard_map/finish/pallas_call | solution.py:259
  (56 shorter events, 4.6 us)
Async XLA Ops:
  0.6 1.7 %collective-permute-start = (bf16[128,512]{1,0:T(8,128)(2,1)}, bf16[128,512]{1,0:T(8,128)(2,1)S(1)}, u32[]{:S(2)}, u32[]{:S(2)}) collective-permute-start(bf16[128,512]{1,0:T(8,128)(2,1)} %param.6), channel_id=1, source_target_pairs={{0,1},{1,0},{2,3},{3,2},{4,5},{5,4},{6,7},{7,6},{8,9},{9,8},{10,11... | collective-permute-start | bytes 393224 | tf_op jit(solution)/shard_map/ppermute | solution.py:291
  1.2 1.6 %collective-permute-start.1 = (bf16[128,512]{1,0:T(8,128)(2,1)}, bf16[128,512]{1,0:T(8,128)(2,1)S(1)}, u32[]{:S(2)}, u32[]{:S(2)}) collective-permute-start(bf16[128,512]{1,0:T(8,128)(2,1)} %param.7), channel_id=1, source_target_pairs={{0,1},{1,0},{2,3},{3,2},{4,5},{5,4},{6,7},{7,6},{8,9},{9,8},{10,11... | collective-permute-start | bytes 393224 | tf_op jit(solution)/shard_map/ppermute | solution.py:291
  2.8 14.7 %collective-permute-start.2 = (bf16[128,4096]{1,0:T(8,128)(2,1)}, bf16[128,4096]{1,0:T(8,128)(2,1)S(1)}, u32[]{:S(2)}, u32[]{:S(2)}) collective-permute-start(bf16[128,4096]{1,0:T(8,128)(2,1)} %refs_2_.1), channel_id=1, source_target_pairs={{0,1},{1,0},{2,3},{3,2},{4,5},{5,4},{6,7},{7,6},{8,9},{9,8},{10,11... | collective-permute-start | bytes 3145736 | tf_op jit(solution)/shard_map/ppermute | solution.py:291
  3.0 15.1 %collective-permute-start.3 = (bf16[128,4096]{1,0:T(8,128)(2,1)}, bf16[128,4096]{1,0:T(8,128)(2,1)S(1)}, u32[]{:S(2)}, u32[]{:S(2)}) collective-permute-start(bf16[128,4096]{1,0:T(8,128)(2,1)} %refs_3_.1), channel_id=1, source_target_pairs={{0,1},{1,0},{2,3},{3,2},{4,5},{5,4},{6,7},{7,6},{8,9},{9,8},{10,11... | collective-permute-start | bytes 3145736 | tf_op jit(solution)/shard_map/ppermute | solution.py:291
  3.4 9.1 %collective-permute-start.4 = (bf16[256,256]{1,0:T(8,128)(2,1)S(1)}, bf16[256,256]{1,0:T(8,128)(2,1)S(1)}, u32[]{:S(2)}, u32[]{:S(2)}) collective-permute-start(bf16[256,256]{1,0:T(8,128)(2,1)S(1)} %maximum_maximum_fusion.refs_0_), channel_id=1, source_target_pairs={{0,8},{8,16},{16,24},{24,0},{1,9},{9,17},{17,25},{25,1},{2,10},{10... | collective-permute-start | bytes 393224 | tf_op jit(solution)/shard_map/ppermute | solution.py:305
  6.2 9.6 %collective-permute-start.11 = (bf16[256,256]{1,0:T(8,128)(2,1)S(1)}, bf16[256,256]{1,0:T(8,128)(2,1)S(1)}, u32[]{:S(2)}, u32[]{:S(2)}) collective-permute-start(bf16[256,256]{1,0:T(8,128)(2,1)S(1)} %maximum_maximum_fusion.1.refs_1_.refs_0_), channel_id=1, source_target_pairs={{0,8},{8,16},{16,24},{24,0},{1,9},{9,17},{17,25},{25,1},{2,10},{10... | collective-permute-start | bytes 393224 | tf_op jit(solution)/shard_map/ppermute | solution.py:305
  12.5 11.4 %collective-permute-start.5 = (bf16[256,256]{1,0:T(8,128)(2,1)S(1)}, bf16[256,256]{1,0:T(8,128)(2,1)S(1)}, u32[]{:S(2)}, u32[]{:S(2)}) collective-permute-start(bf16[256,256]{1,0:T(8,128)(2,1)S(1)} %get-tuple-element.80), channel_id=1, source_target_pairs={{0,2},{1,3},{2,0},{3,1},{4,6},{5,7},{6,4},{7,5},{8,10},{9,11},{10,... | collective-permute-start | bytes 393224 | tf_op jit(solution)/shard_map/ppermute | solution.py:291
  14.3 11.3 %collective-permute-start.6 = (bf16[256,256]{1,0:T(8,128)(2,1)S(1)}, bf16[256,256]{1,0:T(8,128)(2,1)S(1)}, u32[]{:S(2)}, u32[]{:S(2)}) collective-permute-start(bf16[256,256]{1,0:T(8,128)(2,1)S(1)} %get-tuple-element.79), channel_id=1, source_target_pairs={{0,4},{1,5},{2,6},{3,7},{4,0},{5,1},{6,2},{7,3},{8,12},{9,13},{10,... | collective-permute-start | bytes 393224 | tf_op jit(solution)/shard_map/ppermute | solution.py:291
  15.8 9.7 %collective-permute-start.7 = (bf16[256,256]{1,0:T(8,128)(2,1)S(1)}, bf16[256,256]{1,0:T(8,128)(2,1)S(1)}, u32[]{:S(2)}, u32[]{:S(2)}) collective-permute-start(bf16[256,256]{1,0:T(8,128)(2,1)S(1)} %get-tuple-element.78), channel_id=1, source_target_pairs={{0,6},{1,7},{2,4},{3,5},{4,2},{5,3},{6,0},{7,1},{8,14},{9,15},{10,... | collective-permute-start | bytes 393224 | tf_op jit(solution)/shard_map/ppermute | solution.py:291
  17.5 15.3 %collective-permute-start.12 = (bf16[256,256]{1,0:T(8,128)(2,1)S(1)}, bf16[256,256]{1,0:T(8,128)(2,1)S(1)}, u32[]{:S(2)}, u32[]{:S(2)}) collective-permute-start(bf16[256,256]{1,0:T(8,128)(2,1)S(1)} %get-tuple-element.77), channel_id=1, source_target_pairs={{0,2},{1,3},{2,0},{3,1},{4,6},{5,7},{6,4},{7,5},{8,10},{9,11},{10,... | collective-permute-start | bytes 393224 | tf_op jit(solution)/shard_map/ppermute | solution.py:291
  18.1 15.4 %collective-permute-start.13 = (bf16[256,256]{1,0:T(8,128)(2,1)S(1)}, bf16[256,256]{1,0:T(8,128)(2,1)S(1)}, u32[]{:S(2)}, u32[]{:S(2)}) collective-permute-start(bf16[256,256]{1,0:T(8,128)(2,1)S(1)} %get-tuple-element.76), channel_id=1, source_target_pairs={{0,4},{1,5},{2,6},{3,7},{4,0},{5,1},{6,2},{7,3},{8,12},{9,13},{10,... | collective-permute-start | bytes 393224 | tf_op jit(solution)/shard_map/ppermute | solution.py:291
  23.9 9.5 %collective-permute-start.14 = (bf16[256,256]{1,0:T(8,128)(2,1)S(1)}, bf16[256,256]{1,0:T(8,128)(2,1)S(1)}, u32[]{:S(2)}, u32[]{:S(2)}) collective-permute-start(bf16[256,256]{1,0:T(8,128)(2,1)S(1)} %get-tuple-element.75), channel_id=1, source_target_pairs={{0,6},{1,7},{2,4},{3,5},{4,2},{5,3},{6,0},{7,1},{8,14},{9,15},{10,... | collective-permute-start | bytes 393224 | tf_op jit(solution)/shard_map/ppermute | solution.py:291
  26.3 16.4 %collective-permute-start.10 = (bf16[256,256]{1,0:T(8,128)(2,1)S(1)}, bf16[256,256]{1,0:T(8,128)(2,1)S(1)}, u32[]{:S(2)}, u32[]{:S(2)}) collective-permute-start(bf16[256,256]{1,0:T(8,128)(2,1)S(1)} %get-tuple-element.46), channel_id=1, source_target_pairs={{0,6},{1,7},{2,4},{3,5},{4,2},{5,3},{6,0},{7,1},{8,14},{9,15},{10,... | collective-permute-start | bytes 393224 | tf_op jit(solution)/shard_map/ppermute | solution.py:291
  32.8 9.9 %collective-permute-start.8 = (bf16[256,256]{1,0:T(8,128)(2,1)S(1)}, bf16[256,256]{1,0:T(8,128)(2,1)S(1)}, u32[]{:S(2)}, u32[]{:S(2)}) collective-permute-start(bf16[256,256]{1,0:T(8,128)(2,1)S(1)} %get-tuple-element.44), channel_id=1, source_target_pairs={{0,2},{1,3},{2,0},{3,1},{4,6},{5,7},{6,4},{7,5},{8,10},{9,11},{10,... | collective-permute-start | bytes 393224 | tf_op jit(solution)/shard_map/ppermute | solution.py:291
  32.8 9.9 %collective-permute-start.9 = (bf16[256,256]{1,0:T(8,128)(2,1)S(1)}, bf16[256,256]{1,0:T(8,128)(2,1)S(1)}, u32[]{:S(2)}, u32[]{:S(2)}) collective-permute-start(bf16[256,256]{1,0:T(8,128)(2,1)S(1)} %get-tuple-element.45), channel_id=1, source_target_pairs={{0,4},{1,5},{2,6},{3,7},{4,0},{5,1},{6,2},{7,3},{8,12},{9,13},{10,... | collective-permute-start | bytes 393224 | tf_op jit(solution)/shard_map/ppermute | solution.py:291
  34.2 17.2 %collective-permute-start.16 = (bf16[256,256]{1,0:T(8,128)(2,1)S(1)}, bf16[256,256]{1,0:T(8,128)(2,1)S(1)}, u32[]{:S(2)}, u32[]{:S(2)}) collective-permute-start(bf16[256,256]{1,0:T(8,128)(2,1)S(1)} %get-tuple-element.57), channel_id=1, source_target_pairs={{0,2},{1,3},{2,0},{3,1},{4,6},{5,7},{6,4},{7,5},{8,10},{9,11},{10,... | collective-permute-start | bytes 393224 | tf_op jit(solution)/shard_map/ppermute | solution.py:291
  37.3 14.0 %collective-permute-start.17 = (bf16[256,256]{1,0:T(8,128)(2,1)S(1)}, bf16[256,256]{1,0:T(8,128)(2,1)S(1)}, u32[]{:S(2)}, u32[]{:S(2)}) collective-permute-start(bf16[256,256]{1,0:T(8,128)(2,1)S(1)} %get-tuple-element.58), channel_id=1, source_target_pairs={{0,4},{1,5},{2,6},{3,7},{4,0},{5,1},{6,2},{7,3},{8,12},{9,13},{10,... | collective-permute-start | bytes 393224 | tf_op jit(solution)/shard_map/ppermute | solution.py:291
  42.7 8.6 %collective-permute-start.18 = (bf16[256,256]{1,0:T(8,128)(2,1)S(1)}, bf16[256,256]{1,0:T(8,128)(2,1)S(1)}, u32[]{:S(2)}, u32[]{:S(2)}) collective-permute-start(bf16[256,256]{1,0:T(8,128)(2,1)S(1)} %get-tuple-element.59), channel_id=1, source_target_pairs={{0,6},{1,7},{2,4},{3,5},{4,2},{5,3},{6,0},{7,1},{8,14},{9,15},{10,... | collective-permute-start | bytes 393224 | tf_op jit(solution)/shard_map/ppermute | solution.py:291
  42.9 12.5 %collective-permute-start.22 = (bf16[256,256]{1,0:T(8,128)(2,1)S(1)}, bf16[256,256]{1,0:T(8,128)(2,1)S(1)}, u32[]{:S(2)}, u32[]{:S(2)}) collective-permute-start(bf16[256,256]{1,0:T(8,128)(2,1)S(1)} %fusion.3), channel_id=1, source_target_pairs={{8,0},{16,8},{24,16},{0,24},{9,1},{17,9},{25,17},{1,25},{10,2},{18... | collective-permute-start | bytes 393224 | tf_op jit(solution)/shard_map/ppermute | solution.py:376
  51.5 6.0 %collective-permute-start.21 = (bf16[256,256]{1,0:T(8,128)(2,1)S(1)}, bf16[256,256]{1,0:T(8,128)(2,1)S(1)}, u32[]{:S(2)}, u32[]{:S(2)}) collective-permute-start(bf16[256,256]{1,0:T(8,128)(2,1)S(1)} %fusion.10), channel_id=1, source_target_pairs={{8,0},{16,8},{24,16},{0,24},{9,1},{17,9},{25,17},{1,25},{10,2},{18... | collective-permute-start | bytes 393224 | tf_op jit(solution)/shard_map/ppermute | solution.py:376
  52.9 2.9 %collective-permute-start.15 = (bf16[128,1024]{1,0:T(8,128)(2,1)S(1)}, bf16[128,1024]{1,0:T(8,128)(2,1)S(1)}, u32[]{:S(2)}, u32[]{:S(2)}) collective-permute-start(bf16[128,1024]{1,0:T(8,128)(2,1)S(1)} %get-tuple-element.54), channel_id=1, source_target_pairs={{0,1},{1,0},{2,3},{3,2},{4,5},{5,4},{6,7},{7,6},{8,9},{9,8},{10,11... | collective-permute-start | bytes 786440 | tf_op jit(solution)/shard_map/ppermute | solution.py:291
  54.6 1.7 %collective-permute-start.19 = (bf16[128,1024]{1,0:T(8,128)(2,1)S(1)}, bf16[128,1024]{1,0:T(8,128)(2,1)S(1)}, u32[]{:S(2)}, u32[]{:S(2)}) collective-permute-start(bf16[128,1024]{1,0:T(8,128)(2,1)S(1)} %get-tuple-element.63), channel_id=1, source_target_pairs={{0,1},{1,0},{2,3},{3,2},{4,5},{5,4},{6,7},{7,6},{8,9},{9,8},{10,11... | collective-permute-start | bytes 786440 | tf_op jit(solution)/shard_map/ppermute | solution.py:291
  55.2 2.2 %collective-permute-start.20 = (f32[2,128,256]{2,1,0:T(8,128)S(1)}, f32[2,128,256]{2,1,0:T(8,128)S(1)}, u32[]{:S(2)}, u32[]{:S(2)}) collective-permute-start(f32[2,128,256]{2,1,0:T(8,128)S(1)} %pad_maximum_fusion.1), channel_id=1, source_target_pairs={{0,1},{1,0},{2,3},{3,2},{4,5},{5,4},{6,7},{7,6},{8,9},{9,8},{10,11... | collective-permute-start | bytes 786440 | tf_op jit(solution)/shard_map/ppermute | solution.py:291
  55.3 2.5 %collective-permute-start.23 = (bf16[256,256]{1,0:T(8,128)(2,1)S(1)}, bf16[256,256]{1,0:T(8,128)(2,1)S(1)}, u32[]{:S(2)}, u32[]{:S(2)}) collective-permute-start(bf16[256,256]{1,0:T(8,128)(2,1)S(1)} %collective-permute-done.22.refs_2_), channel_id=1, source_target_pairs={{0,1},{1,0},{2,3},{3,2},{4,5},{5,4},{6,7},{7,6},{8,9},{9,8},{10,11... | collective-permute-start | bytes 393224 | tf_op jit(solution)/shard_map/ppermute | solution.py:291
  (4 other events, 23.6 us)
